TPU v7x, 128 devices: a whole 4x4x4 slice. The times are simulated.
128 devices in a mesh: dp: 32 (over x, y, core), tp: 4 (over z).
Axes of the slice: x: 4, y: 4, z: 4, core: 2. Of those that a mesh axis runs over, the one named last changes fastest.
Arguments:
- query: bfloat16 [128, 64, 576], P('dp', 'tp'), may hold values from -65 to 65
- new_latent: bfloat16 [128, 576], P('dp'), may hold values from -4 to 4
- cache: bfloat16 [64, 1024, 576], P('dp'), may hold values from -4 to 4
- cache_len: int32 [64], P('dp'), may hold values from 128 to 1024, as said below
- w_uv: bfloat16 [64, 512, 128], P('tp'), may hold values from -1.5 to 1.5
- w_out: bfloat16 [8192, 7168], P('tp', 'dp'), may hold values from -0.0625 to 0.0625
- hidden_in: bfloat16 [128, 7168], P('tp', 'dp'), may hold values from -25 to 25
- norm_gain: float32 [7168], P('dp'), may hold values from 0.1 to 1.9
- routing: int32 [128, 8], replicated, may hold values from 0 to 15, all different within a row; in each aligned block of 32 rows (0 to 31, 32 to 63, ...) at most 24 rows name the same one
- route_weight: float32 [128, 8], replicated, may hold values from 0.1 to 0.6
- w_gate_up: bfloat16 [2, 7168, 32768], P(None, None, ('dp', 'tp')), may hold values from -0.0625 to 0.0625
- w_down: bfloat16 [32768, 7168], P(('dp', 'tp')), may hold values from -0.125 to 0.125
Outputs:
- hidden_out: bfloat16 [128, 7168], P('tp', 'dp')
Inputs may be any that keep to these rules, and one draw needn't show every extreme that they name: `routing`: each row names 8 different experts. Within each aligned block of 32 rows no expert is named by more than 24 rows, a bound that some block reaches. `cache_len`: some request holds a full cache of 1024 tokens.
All inputs are finite; a program needn't handle non-finite values.
Results may differ from a plain program's by a relative error of at most 0.006.
Values may be sent and summed in bfloat16 or wider, within the bound.
A program may use at most 128 MiB of HBM per device.

v0:
```python
import jax
import jax.numpy as jnp
import numpy as np
from jax import lax
from jax.sharding import PartitionSpec as P

D = 7168
ROPE = 64
VH = 128
EXPERTS = 16


EPSILON = 1e-06


def expert_block(tokens_in, w_gate_up, w_down):
    gate_part = jnp.dot(tokens_in, w_gate_up[0], preferred_element_type=jnp.float32)
    up_part = jnp.dot(tokens_in, w_gate_up[1], preferred_element_type=jnp.float32)
    hidden_act = (jax.nn.silu(gate_part) * up_part).astype(jnp.bfloat16)
    return jnp.dot(hidden_act, w_down, preferred_element_type=jnp.float32)


def on_device(
    query,
    new_latent,
    cache,
    cache_len,
    w_uv,
    w_out,
    hidden_in,
    norm_gain,
    routing,
    route_weight,
    w_gate_up,
    w_down,
):
    dp_count = lax.axis_size("dp")
    tp_count = lax.axis_size("tp")
    tp_index = lax.axis_index("tp")
    device_count = dp_count * tp_count
    req_local = cache.shape[0]
    max_len = cache.shape[1]
    latent = cache.shape[2]
    heads_local = query.shape[1]
    value_width = w_uv.shape[1]
    head_width = w_uv.shape[2]
    col_width = w_out.shape[1]
    scale = float(VH + ROPE) ** (-0.5)
    queries = query.reshape(req_local, 2, heads_local, latent)
    fresh = new_latent.reshape(req_local, 2, latent)
    far_score = (
        jnp.einsum("bthc,blc->bthl", queries, cache, preferred_element_type=jnp.float32) * scale
    )
    live = lax.broadcasted_iota(jnp.int32, (req_local, max_len), 1) < cache_len[:, None]
    far_score = jnp.where(live[:, None, None, :], far_score, -jnp.inf)
    near_score = (
        jnp.einsum("bthc,buc->bthu", queries, fresh, preferred_element_type=jnp.float32) * scale
    )
    causal = lax.broadcasted_iota(jnp.int32, (2, 2), 0) >= lax.broadcasted_iota(
        jnp.int32, (2, 2), 1
    )
    near_score = jnp.where(causal[None, :, None, :], near_score, -jnp.inf)
    highest = jnp.maximum(jnp.max(far_score, axis=-1), jnp.max(near_score, axis=-1))[..., None]
    far_weight = jnp.exp(far_score - highest)
    near_weight = jnp.exp(near_score - highest)
    denominator = (jnp.sum(far_weight, axis=-1) + jnp.sum(near_weight, axis=-1))[..., None]
    far_prob = (far_weight / denominator).astype(jnp.bfloat16)
    near_prob = (near_weight / denominator).astype(jnp.bfloat16)
    context = jnp.einsum(
        "bthl,blc->bthc", far_prob, cache[:, :, :value_width], preferred_element_type=jnp.float32
    )
    context = context + jnp.einsum(
        "bthu,buc->bthc", near_prob, fresh[:, :, :value_width], preferred_element_type=jnp.float32
    )
    context = context.astype(jnp.bfloat16).reshape(2 * req_local, heads_local, value_width)
    head_out = jnp.einsum("ihc,hcv->ihv", context, w_uv, preferred_element_type=jnp.float32)
    head_out = head_out.astype(jnp.bfloat16).reshape(2 * req_local, heads_local * head_width)
    partial_out = jnp.dot(
        lax.all_gather(head_out, "dp", axis=0, tiled=True),
        w_out,
        preferred_element_type=jnp.float32,
    )
    attn_part = lax.psum_scatter(partial_out, "tp", scatter_dimension=0, tiled=True)
    mid = hidden_in.astype(jnp.float32) + attn_part
    square_sum = lax.psum(jnp.sum(mid * mid, axis=1), "dp")
    normed = (mid * lax.rsqrt(square_sum / D + EPSILON)[:, None] * norm_gain[None, :]).astype(
        jnp.bfloat16
    )
    quarter = mid.shape[0]
    capacity = 3 * quarter // 4
    row_start = tp_index * quarter
    my_routes = lax.dynamic_slice_in_dim(routing, row_start, quarter, 0)
    my_weights = lax.dynamic_slice_in_dim(route_weight, row_start, quarter, 0)
    expert_ids = lax.broadcasted_iota(jnp.int32, (1, 1, EXPERTS), 2)
    chosen = my_routes[:, :, None] == expert_ids
    member = jnp.sum(chosen.astype(jnp.int32), axis=1).T
    mixing = jnp.sum(jnp.where(chosen, my_weights[:, :, None], 0.0), axis=1).T
    position = jnp.cumsum(member, axis=1) - 1
    slot_ids = lax.broadcasted_iota(jnp.int32, (1, capacity, 1), 1)
    placed = (member[:, None, :] == 1) & (position[:, None, :] == slot_ids)
    dispatch_rows = jnp.einsum(
        "eci,id->ecd", placed.astype(jnp.bfloat16), normed, preferred_element_type=jnp.float32
    ).astype(jnp.bfloat16)
    combine_map = jnp.where(placed, mixing[:, None, :], 0.0)
    device_table = np.arange(device_count) * EXPERTS // device_count
    outgoing = dispatch_rows[device_table]
    arrived = lax.all_to_all(outgoing, ("dp", "tp"), split_axis=0, concat_axis=0, tiled=True)
    full_rows = arrived.reshape(dp_count, tp_count, capacity, col_width).transpose(1, 2, 0, 3)
    full_rows = full_rows.reshape(tp_count * capacity, dp_count * col_width)
    expert_out = expert_block(full_rows, w_gate_up, w_down)
    outgoing_sums = expert_out.reshape(tp_count, capacity, dp_count, col_width).transpose(
        2, 0, 1, 3
    )
    outgoing_sums = outgoing_sums.reshape(device_count, capacity, col_width)
    returned = lax.all_to_all(outgoing_sums, ("dp", "tp"), split_axis=0, concat_axis=0, tiled=True)
    group_size = device_count // EXPERTS
    summed = jnp.sum(returned.reshape(EXPERTS, group_size, capacity, col_width), axis=1)
    moe_out = jnp.einsum("eci,ecd->id", combine_map, summed, precision=lax.Precision.HIGHEST)
    return (mid + moe_out).astype(jnp.bfloat16)


def solution(mesh):
    placed = (
        P("dp", "tp", None),
        P("dp", None),
        P("dp", None, None),
        P("dp"),
        P("tp", None, None),
        P("tp", "dp"),
        P("tp", "dp"),
        P("dp"),
        P(),
        P(),
        P(None, None, ("dp", "tp")),
        P(("dp", "tp"), None),
    )
    return jax.shard_map(
        on_device, mesh=mesh, in_specs=placed, out_specs=P("tp", "dp"), check_vma=False
    )
```

profile of v0, /device:TPU:1, one launch (start us, length us, event | category | flops | bytes accessed | tf_op | source)
XLA Modules:
  0.0 243.6 jit_solution(7760489888673171675)
XLA Ops:
  6.5 0.0 copy-start
  6.5 0.0 reduce-scatter.2.cloned.1.call-start
  6.5 0.9 reshape.94
  7.4 0.7 reshape.74
  8.1 0.9 iota_compare_fusion.2
  9.0 2.3 fusion.61
  11.3 0.0 copy-done.4
  11.3 0.2 fusion.62
  11.6 0.2 fusion.31
  11.8 0.0 copy-done.1
  11.9 0.7 fusion.8
  12.6 0.2 fusion.17
  12.8 0.0 copy-done
  12.8 0.0 copy-start.5
  12.8 0.0 copy-start.8
  12.9 0.0 copy-start.3
  12.9 0.0 copy-start.7
  12.9 0.4 fusion.28
  13.3 26.4 %all-gather = bf16[32,4,2048]{2,1,0:T(4,128)(2,1)S(1)} all-gather(bf16[1,4,2048]{2,1,0:T(4,128)(2,1)S(1)} %fusion.28), channel_id=1, replica_groups=mesh['dp'=32,'tp'=4] {'dp'}, dimensions={0}, use_global_device_ids=true | all-gather | bytes 540672 | tf_op jit(solution)/shard_map/all_gather | solution.py:79
  39.7 0.1 reshape.91
  39.8 2.3 fusion.63
  42.1 0.0 reduce-scatter.2.cloned.1.call-update
  42.1 0.0 copy-done.5
  42.1 0.1 constant_dynamic-slice_fusion.1
  42.2 0.0 copy-done.8
  42.3 0.2 reduce_window_sum.11
  42.5 18.0 %reduce-scatter.2.cloned.1.call-done = f32[32,224]{1,0:T(8,128)} async-done(((f32[128,224]{1,0:T(8,128)}), f32[32,224]{1,0:T(8,128)}) %reduce-scatter.2.cloned.1.call-update) | async-done | bytes 28688 | tf_op jit(solution)/shard_map/reduce_scatter | solution.py:83
  60.5 0.0 copy-done.3
  60.5 0.9 multiply_reduce_fusion
  61.3 65.0 %psum.7 = f32[32]{0:T(128)S(1)} all-reduce(f32[32]{0:T(128)S(1)} %multiply_reduce_fusion), channel_id=1, replica_groups=mesh['dp'=32,'tp'=4] {'dp'}, use_global_device_ids=true, to_apply=%region_9.10 | all-reduce | flops 32 | bytes 256 | tf_op jit(solution)/shard_map/psum | solution.py:85
  126.3 0.0 copy-done.7
  126.3 1.0 convolution_convert_fusion
  127.3 1.8 gather_fusion
  129.1 31.7 %all_to_all.10 = bf16[128,24,224]{2,1,0:T(8,128)(2,1)S(1)} all-to-all(bf16[128,24,224]{2,1,0:T(8,128)(2,1)} %gather_fusion), channel_id=1, replica_groups=mesh['dp'=32,'tp'=4] {'dp','tp'}, dimensions={0} | all-to-all | bytes 2752512 | tf_op jit(solution)/shard_map/all_to_all | solution.py:107
  160.8 2.0 copy.43
  162.9 3.4 %reshape.78 = bf16[96,7168]{1,0:T(8,128)(2,1)S(1)} reshape(bf16[4,24,32,224]{3,2,1,0:T(8,128)(2,1)} %bitcast.79) | data formatting | bytes 2752512 | tf_op jit(solution)/shard_map/reshape | solution.py:109
  166.3 3.4 %fusion.2 = f32[96,256]{1,0:T(8,128)} fusion(bf16[96,7168]{1,0:T(8,128)(2,1)S(1)} %reshape.78, bf16[2,7168,256]{2,1,0:T(8,128)(2,1)} %param.24), kind=kOutput, calls=%fused_computation.3 | convolution fusion | flops 352321536 | bytes 5144576 | tf_op jit(solution)/shard_map/dot_general | solution.py:17
  169.7 6.9 %fusion.25 = f32[96,7168]{1,0:T(8,128)} fusion(bf16[256,7168]{1,0:T(8,128)(2,1)} %param.25, bf16[96,7168]{1,0:T(8,128)(2,1)S(1)} %reshape.78, bf16[2,7168,256]{2,1,0:T(8,128)(2,1)} %param.24, f32[96,256]{1,0:T(8,128)} %fusion.2), kind=kOutput, calls=%fused_computation.21 | convolution fusion | flops 704790528 | bytes 11567104 | tf_op jit(solution)/shard_map/dot_general | solution.py:20
  176.6 4.6 %reshape.79 = f32[4,24,32,224]{3,2,1,0:T(8,128)} reshape(f32[96,7168]{1,0:T(8,128)} %fusion.25) | data formatting | bytes 5505024 | tf_op jit(solution)/shard_map/reshape | solution.py:111
  181.2 5.4 %copy.34 = f32[4,24,32,224]{3,1,0,2:T(8,128)} copy(f32[4,24,32,224]{3,2,1,0:T(8,128)} %reshape.79) | data formatting | bytes 5505024 | tf_op jit(solution)/shard_map/reshape | solution.py:111
  186.6 5.0 %all-to-all-start.1 = ((f32[128,24,224]{2,1,0:T(8,128)}), f32[128,24,224]{2,1,0:T(8,128)}, u32[]{:S(2)}, u32[]{:S(2)}) async-start(f32[128,24,224]{2,1,0:T(8,128)} %bitcast.77), calls=%async_computation.2 | async-start | bytes 6291456 | tf_op jit(solution)/shard_map/all_to_all | solution.py:115
  191.6 0.0 copy-done.6
  191.6 0.0 copy-start.2
  191.6 0.1 constant_dynamic-slice_fusion
  191.7 41.8 %all-to-all-done.1 = f32[128,24,224]{2,1,0:T(8,128)} async-done(((f32[128,24,224]{2,1,0:T(8,128)}), f32[128,24,224]{2,1,0:T(8,128)}, u32[]{:S(2)}, u32[]{:S(2)}) %all-to-all-start.1) | async-done | bytes 2752544 | tf_op jit(solution)/shard_map/all_to_all | solution.py:115
  233.5 2.2 bitcast_reduce_fusion
  235.7 0.0 copy-done.2
  235.7 1.1 fusion.29
  (13 shorter events, 0.1 us)
Async XLA Ops:
  6.5 6.3 %copy-start = (bf16[16,512,128]{2,1,0:T(8,128)(2,1)S(1)}, bf16[16,512,128]{2,1,0:T(8,128)(2,1)}, u32[]{:S(2)}) copy-start(bf16[16,512,128]{2,1,0:T(8,128)(2,1)} %param.18) | copy-start | bytes 6291460
  6.5 4.8 %copy-start.4 = (bf16[4,16,576]{2,1,0:T(8,128)(2,1)S(1)}, bf16[4,16,576]{2,1,0:T(8,128)(2,1)}, u32[]{:S(2)}) copy-start(bf16[4,16,576]{2,1,0:T(8,128)(2,1)} %param.14) | copy-start | bytes 221188
  6.5 53.9 %reduce-scatter.2.cloned.1.call-start = ((), (), s32[]{:S(2)}) async-start(), calls=%async_computation.3 | async-start | bytes 163840 | tf_op jit(solution)/shard_map/reduce_scatter | solution.py:83
  8.1 3.7 %copy-start.1 = (bf16[2,1024,576]{1,2,0:T(8,128)(2,1)S(1)}, bf16[2,1024,576]{1,2,0:T(8,128)(2,1)}, u32[]{:S(2)}) copy-start(bf16[2,1024,576]{1,2,0:T(8,128)(2,1)} %param.16) | copy-start | bytes 7077892
  12.8 29.3 %copy-start.5 = (s32[128,8]{0,1:T(8,128)S(1)}, s32[128,8]{0,1:T(8,128)}, u32[]{:S(2)}) copy-start(s32[128,8]{0,1:T(8,128)} %param.22) | copy-start | bytes 12292
  12.8 29.4 %copy-start.8 = (s32[128]{0:T(128)S(1)}, s32[128]{0:T(128)}, u32[]{:S(2)}) copy-start(s32[128]{0:T(128)} %constant.46) | copy-start | bytes 1540
  12.9 47.6 %copy-start.3 = (bf16[32,224]{1,0:T(8,128)(2,1)S(1)}, bf16[32,224]{1,0:T(8,128)(2,1)}, u32[]{:S(2)}) copy-start(bf16[32,224]{1,0:T(8,128)(2,1)} %param.20) | copy-start | bytes 43012
  12.9 113.4 %copy-start.7 = (f32[224]{0:T(256)S(1)}, f32[224]{0:T(256)}, u32[]{:S(2)}) copy-start(f32[224]{0:T(256)} %param.21) | copy-start | bytes 2692
  186.6 5.0 %copy-start.6 = (f32[128,8]{0,1:T(8,128)S(1)}, f32[128,8]{0,1:T(8,128)}, u32[]{:S(2)}) copy-start(f32[128,8]{0,1:T(8,128)} %param.23) | copy-start | bytes 12292
  186.6 46.9 %all-to-all-start.1 = ((f32[128,24,224]{2,1,0:T(8,128)}), f32[128,24,224]{2,1,0:T(8,128)}, u32[]{:S(2)}, u32[]{:S(2)}) async-start(f32[128,24,224]{2,1,0:T(8,128)} %bitcast.77), calls=%async_computation.2 | async-start | bytes 6291456 | tf_op jit(solution)/shard_map/all_to_all | solution.py:115
  191.6 44.1 %copy-start.2 = (f32[32,224]{1,0:T(8,128)S(1)}, f32[32,224]{1,0:T(8,128)}, u32[]{:S(2)}) copy-start(f32[32,224]{1,0:T(8,128)} %reduce-scatter.2.cloned.1.call-done) | copy-start | bytes 86020
Sparse Core Ops, SparseCore 0:
  42.2 18.1 reduce-scatter.1
where the time goes:
time: 244 us
  blocking collectives  123 us (50%)
  waiting for transfers between devices  59.8 us (25%)
  local copies, waits for them, and re-layouts  19.2 us (8%)
  matrix products  18.6 us (8%)
  between operations  13.6 us (6%)
  starting transfers between devices  4.99 us (2%)
  other arithmetic  4.41 us (2%)
    psum x1, blocking collectives, on_device(): square_sum = lax.psum(jnp.sum(mid * mid, axis=1), 'dp')  65 us
    all_to_all x1, waiting for transfers between devices, on_device(): lax.all_to_all(outgoing_sums, ('dp', 'tp'), split_axis=0, concat_axis=0,...  41.8 us
    all_to_all x1, blocking collectives, on_device(): lax.all_to_all(outgoing, ('dp', 'tp'), split_axis=0, concat_axis=0, tiled...  31.7 us
    all_gather x1, blocking collectives, on_device(): lax.all_gather(head_out, 'dp', axis=0, tiled=True)  26.4 us
    reduce_scatter x1, waiting for transfers between devices, on_device(): lax.psum_scatter(partial_out, 'tp', scatter_dimension=0, tiled=True)  18 us
    reshape x2, local copies, waits for them, and re-layouts, on_device(): expert_out.reshape(tp_count, capacity, dp_count, col_width)  10 us
    dot_general x1, matrix products, expert_block(): return jnp.dot(hidden_act, w_down, preferred_element_type=jnp.float32)  6.9 us
    all_to_all x1, starting transfers between devices, on_device(): lax.all_to_all(outgoing_sums, ('dp', 'tp'), split_axis=0, concat_axis=0,...  4.99 us
  transfers between devices with their start and end apart: 2, of which 2 were waited for; matrix products, arithmetic and copies ran while one was open for 0% of the time, Pallas kernels for 0%

commit v1 on v0

v1 whole, which is shorter than its diff:
```python
import jax
import jax.numpy as jnp
from jax import lax
from jax.experimental import pallas as pl
from jax.experimental.pallas import tpu as pltpu
from jax.sharding import PartitionSpec as P

D = 7168
LAT = 576
KVL = 512
ROPE = 64
VH = 128
MAXLEN = 1024
EXPERTS = 16
TOKENS = 128
TOP = 8
QTOK = 32
CAP = 24
ROWS = 4 * CAP
COLS = 224
WIDE = 256
UNITS = 256
XY = 16
EPSILON = 1e-06
MESH = pl.DeviceIdType.MESH
F32 = jnp.float32
BF16 = jnp.bfloat16


def mm(a, b, dims=((1,), (0,)), precision=None):
    return lax.dot_general(a, b, (dims, ((), ())), preferred_element_type=F32, precision=precision)


def kernel(
    query, new_latent, cache, cache_len, w_uv, w_out, hidden_in, gain, routing, route_weight,
    w_gate_up, w_down, out,
    cache_v, uv_v, out_v, gu_v, down_v,
    heads, heads32, part, part_in, rows_z, pick, pick_t, mem_t, pos_t, mid_s, wcol,
    x_out, x_in, gate_s, up_s, sq_s, act_s, y_mine, y_sib, y_out, y_in, fin, fin_in,
    load_sem, a_s, a_r, a2_s, a2_r, c_s, c_r, d_s, d_r, e_s, e_r, e2_s, e2_r,
    g_s, g_r, g2_s, g2_r, h_s, h_r,
):
    dp = lax.axis_index("dp")
    z = lax.axis_index("tp")
    xy = dp // 2
    core = dp % 2
    sib = xy * 2 + (1 - core)

    def peer(k):
        return (xy + k) % XY

    def source(k):
        return (xy + XY - k) % XY

    def zpeer(j):
        return (z + j) % 4

    def remote(src, dst, send, recv, to_dp, to_z):
        return pltpu.make_async_remote_copy(
            src_ref=src, dst_ref=dst, send_sem=send, recv_sem=recv,
            device_id=(to_dp, to_z), device_id_type=MESH,
        )

    barrier = pltpu.get_barrier_semaphore()

    def greet(k, _):
        pl.semaphore_signal(barrier, inc=1, device_id=(peer(k) * 2 + core, z), device_id_type=MESH)
        return 0

    pl.semaphore_signal(barrier, inc=1, device_id=(sib, z), device_id_type=MESH)
    lax.fori_loop(1, XY, greet, 0)
    for j in range(1, 4):
        pl.semaphore_signal(barrier, inc=1, device_id=(dp, zpeer(j)), device_id_type=MESH)

    loads = [
        pltpu.make_async_copy(cache.at[0], cache_v.at[0], load_sem.at[0]),
        pltpu.make_async_copy(cache.at[1], cache_v.at[1], load_sem.at[1]),
        pltpu.make_async_copy(w_uv, uv_v, load_sem.at[2]),
        pltpu.make_async_copy(w_out, out_v, load_sem.at[3]),
        pltpu.make_async_copy(w_gate_up, gu_v, load_sem.at[4]),
        pltpu.make_async_copy(w_down, down_v, load_sem.at[5]),
    ]
    for copy in loads:
        copy.start()

    scale = float(VH + ROPE) ** (-0.5)
    q_all = query[...].reshape(4 * XY, LAT)
    fresh = new_latent[...]
    near = mm(q_all, fresh, ((1,), (1,))) * scale
    row = lax.broadcasted_iota(jnp.int32, (64, 4), 0)
    col = lax.broadcasted_iota(jnp.int32, (64, 4), 1)
    near = jnp.where((row // 32 == col // 2) & (row // 16 >= col), near, -jnp.inf)
    contexts = []
    for b in range(2):
        loads[b].wait()
        q = q_all[32 * b : 32 * b + 32]
        far = mm(q, cache_v[b], ((1,), (1,))) * scale
        place = lax.broadcasted_iota(jnp.int32, (32, MAXLEN), 1)
        far = jnp.where(place < cache_len[b], far, -jnp.inf)
        close = near[32 * b : 32 * b + 32]
        highest = jnp.maximum(
            jnp.max(far, axis=1, keepdims=True), jnp.max(close, axis=1, keepdims=True)
        )
        far = jnp.exp(far - highest)
        close = jnp.exp(close - highest)
        total = jnp.sum(far, axis=1, keepdims=True) + jnp.sum(close, axis=1, keepdims=True)
        context = mm((far / total).astype(BF16), cache_v[b, :, :KVL])
        context = context + mm((close / total).astype(BF16), fresh[:, :KVL])
        contexts.append(context.astype(BF16))
    context = jnp.concatenate(contexts, axis=0)
    loads[2].wait()
    row = lax.broadcasted_iota(jnp.int32, (64, VH), 0)
    head_out = jnp.zeros((64, VH), F32)
    for h in range(16):
        head_out = jnp.where(row % 16 == h, mm(context, uv_v[h]), head_out)
    heads[dp] = head_out.astype(BF16)

    pl.semaphore_wait(barrier, XY + 3)

    def a_copy(k):
        return remote(heads.at[dp], heads.at[dp], a_s.at[k], a_r.at[k], peer(k) * 2 + core, z)

    def a2_copy(k):
        which = source(k) * 2 + core
        return remote(heads.at[which], heads.at[which], a2_s.at[k], a2_r.at[k], sib, z)

    def a_start(k, _):
        a_copy(k).start()
        return 0

    lax.fori_loop(1, XY, a_start, 0)
    a2_copy(0).start()

    lane16 = lax.broadcasted_iota(jnp.int32, (TOKENS, EXPERTS), 1)
    member = jnp.zeros((TOKENS, EXPERTS), F32)
    share = jnp.zeros((TOKENS, 1), F32)
    for k in range(TOP):
        named = routing[:, k : k + 1]
        member = member + jnp.where(named == lane16, 1.0, 0.0)
        share = share + jnp.where(named == xy, route_weight[:, k : k + 1], 0.0)
    member = member.astype(BF16)
    i0 = lax.broadcasted_iota(jnp.int32, (TOKENS, TOKENS), 0)
    i1 = lax.broadcasted_iota(jnp.int32, (TOKENS, TOKENS), 1)
    eye = jnp.where(i0 == i1, 1.0, 0.0).astype(BF16)
    earlier = jnp.where((i0 < i1) & (i0 // QTOK == i1 // QTOK), 1.0, 0.0).astype(BF16)
    mem_t[...] = mm(member, eye, ((0,), (0,)))
    pos_t[...] = mm(member, earlier, ((0,), (0,)))
    slot = lax.broadcasted_iota(jnp.int32, (ROWS, TOKENS), 0)
    token = lax.broadcasted_iota(jnp.int32, (ROWS, TOKENS), 1)
    in_block = slot // CAP == token // QTOK
    rank = (slot % CAP).astype(F32)

    def tables(e, _):
        here = (mem_t[pl.ds(e, 1), :] > 0.5) & in_block & (pos_t[pl.ds(e, 1), :] == rank)
        chosen = jnp.where(here, 1.0, 0.0).astype(BF16)
        pick[e] = chosen
        pick_t[e] = mm(eye, chosen, ((1,), (1,))).astype(BF16)
        return 0

    lax.fori_loop(0, EXPERTS, tables, 0)
    wcol[...] = mm(
        pick[xy].astype(F32), jnp.broadcast_to(share, (TOKENS, 128)), precision=lax.Precision.HIGHEST
    )

    def a_forward(k, _):
        a_copy(k).wait_recv()
        a2_copy(k).start()
        return 0

    lax.fori_loop(1, XY, a_forward, 0)

    def a_finish(k, _):
        a2_copy(k).wait_recv()
        return 0

    lax.fori_loop(0, XY, a_finish, 0)

    heads32[...] = heads[...].reshape(32 * 64, VH).astype(F32)
    loads[3].wait()
    projected = jnp.zeros((TOKENS, COLS), F32)
    for h in range(16):
        lhs = heads32[pl.ds(h, TOKENS, stride=16), :].astype(BF16)
        projected = projected + mm(lhs, out_v[VH * h : VH * (h + 1), :])
    for q in range(4):
        part[q, :, :COLS] = projected[QTOK * q : QTOK * (q + 1)]
        part[q, :, COLS:] = jnp.zeros((QTOK, WIDE - COLS), F32)

    def c_copy(j):
        return remote(part.at[zpeer(j)], part_in.at[z], c_s.at[j], c_r.at[j], dp, zpeer(j))

    for j in range(1, 4):
        c_copy(j).start()
    mid = part[z][:, :COLS] + hidden_in[...].astype(F32)
    for j in range(1, 4):
        c_copy(j).wait_recv()
        mid = mid + part_in[zpeer(4 - j)][:, :COLS]
    mid_s[...] = mid
    square = jnp.sum(mid * mid, axis=1, keepdims=True)
    square_hi = square.astype(BF16)
    square_lo = (square - square_hi.astype(F32)).astype(BF16)
    rows_z[z, :, :COLS] = (mid * gain[...]).astype(BF16)
    lane = lax.broadcasted_iota(jnp.int32, (QTOK, WIDE - COLS), 1)
    spare = jnp.where(lane == 0, square_hi.astype(F32), jnp.where(lane == 1, square_lo.astype(F32), 0.0))
    rows_z[z, :, COLS:] = spare.astype(BF16)

    def d_copy(j):
        return remote(rows_z.at[z], rows_z.at[z], d_s.at[j], d_r.at[j], dp, zpeer(j))

    for j in range(1, 4):
        d_copy(j).start()
    for j in range(1, 4):
        remote(rows_z.at[zpeer(j)], rows_z.at[zpeer(4 - j)], d_s.at[j], d_r.at[j], dp, zpeer(j)).wait_recv()

    def e_copy(k):
        return remote(x_out.at[k], x_in.at[dp], e_s.at[k], e_r.at[k], peer(k) * 2 + core, z)

    def e2_copy(k):
        which = source(k) * 2 + core
        return remote(x_in.at[which], x_in.at[which], e2_s.at[k], e2_r.at[k], sib, z)

    all_rows = rows_z[...].reshape(TOKENS, WIDE)

    def e_start(k, _):
        x_out[k] = mm(pick[peer(k)], all_rows).astype(BF16)
        e_copy(k).start()
        return 0

    lax.fori_loop(1, XY, e_start, 0)
    x_in[dp] = mm(pick[xy], all_rows).astype(BF16)
    e2_copy(0).start()
    loads[4].wait()

    gate_s[...] = jnp.zeros_like(gate_s)
    up_s[...] = jnp.zeros_like(up_s)
    sq_s[...] = jnp.zeros_like(sq_s)

    def take(which):
        x = x_in[which]
        at = pl.ds(pl.multiple_of(which * COLS, COLS), COLS)
        gate_s[...] += mm(x[:, :COLS], gu_v[0, at, :])
        up_s[...] += mm(x[:, :COLS], gu_v[1, at, :])
        sq_s[...] += x[:, 128:].astype(F32)

    take(dp)

    def e_take(k, _):
        e_copy(k).wait_recv()
        e2_copy(k).start()
        take(source(k) * 2 + core)
        return 0

    lax.fori_loop(1, XY, e_take, 0)

    def e2_take(k, _):
        e2_copy(k).wait_recv()
        take(source(k) * 2 + 1 - core)
        return 0

    lax.fori_loop(0, XY, e2_take, 0)
    square = sq_s[:, COLS - 128 : COLS - 127] + sq_s[:, COLS - 127 : COLS - 126]
    factor = lax.rsqrt(square / D + EPSILON)
    g = gate_s[...] * factor
    u = up_s[...] * factor
    act_s[...] = (g / (1.0 + jnp.exp(-g)) * u).astype(BF16)
    loads[5].wait()
    weight = wcol[:, :1]

    def g_copy(t):
        return remote(y_mine.at[t, 1 - core], y_sib.at[t], g_s.at[t], g_r.at[t], sib, z)

    def results(n, _):
        group = ((xy + 1) // 2 + n) % 8
        at = pl.ds(pl.multiple_of(group * 4 * COLS, 128), 4 * COLS)
        y = mm(act_s[...], down_v[:, at]) * weight
        for k in range(4):
            y_mine[group * 2 + k // 2, k % 2, :, :COLS] = y[:, COLS * k : COLS * (k + 1)].astype(BF16)
        g_copy(group * 2).start()
        g_copy(group * 2 + 1).start()
        return 0

    def blank(n, _):
        for k in range(2):
            y_mine[n, k, :, 128:] = jnp.zeros((ROWS, 128), BF16)
        return 0

    lax.fori_loop(0, XY, blank, 0)
    lax.fori_loop(0, 8, results, 0)

    def g2_copy(k):
        return remote(y_out.at[k], y_in.at[xy], g2_s.at[k], g2_r.at[k], peer(k) * 2 + core, z)

    def both(t):
        g_copy(t).wait_recv()
        return (y_mine[t, core].astype(F32) + y_sib[t].astype(F32)).astype(BF16)

    def g2_start(k, _):
        y_out[k] = both(peer(k))
        g2_copy(k).start()
        return 0

    lax.fori_loop(1, XY, g2_start, 0)
    total = mm(pick_t[xy], both(xy))

    def combine(k, total):
        from_xy = source(k)
        remote(y_out.at[k], y_in.at[from_xy], g2_s.at[k], g2_r.at[k], peer(k) * 2 + core, z).wait_recv()
        return total + mm(pick_t[from_xy], y_in[from_xy])

    total = lax.fori_loop(1, XY, combine, total)
    for q in range(4):
        fin[q] = total[QTOK * q : QTOK * (q + 1)]

    def h_copy(j):
        return remote(fin.at[zpeer(j)], fin_in.at[z], h_s.at[j], h_r.at[j], dp, zpeer(j))

    for j in range(1, 4):
        h_copy(j).start()
    result = fin[z][:, :COLS] + mid_s[...]
    for j in range(1, 4):
        remote(fin.at[zpeer(j)], fin_in.at[zpeer(4 - j)], h_s.at[j], h_r.at[j], dp, zpeer(j)).wait_recv()
        result = result + fin_in[zpeer(4 - j)][:, :COLS]
    out[...] = result.astype(BF16)

    def sent(k, _):
        a_copy(k).wait_send()
        e_copy(k).wait_send()
        g2_copy(k).wait_send()
        return 0

    def sent_sib(k, _):
        a2_copy(k).wait_send()
        e2_copy(k).wait_send()
        g_copy(k).wait_send()
        return 0

    lax.fori_loop(1, XY, sent, 0)
    lax.fori_loop(0, XY, sent_sib, 0)
    for j in range(1, 4):
        c_copy(j).wait_send()
        d_copy(j).wait_send()
        h_copy(j).wait_send()


def on_device(
    query, new_latent, cache, cache_len, w_uv, w_out, hidden_in, norm_gain, routing, route_weight,
    w_gate_up, w_down,
):
    vmem = pl.BlockSpec(memory_space=pltpu.VMEM)
    smem = pl.BlockSpec(memory_space=pltpu.SMEM)
    hbm = pl.BlockSpec(memory_space=pl.ANY)
    dma = pltpu.SemaphoreType.DMA
    return pl.pallas_call(
        kernel,
        out_shape=jax.ShapeDtypeStruct((QTOK, COLS), BF16),
        in_specs=[vmem, vmem, hbm, smem, hbm, hbm, vmem, vmem, vmem, vmem, hbm, hbm],
        out_specs=vmem,
        scratch_shapes=[
            pltpu.VMEM((2, MAXLEN, LAT), BF16),
            pltpu.VMEM((16, KVL, VH), BF16),
            pltpu.VMEM((16 * VH, COLS), BF16),
            pltpu.VMEM((2, D, UNITS), BF16),
            pltpu.VMEM((UNITS, D), BF16),
            pltpu.VMEM((32, 64, VH), BF16),
            pltpu.VMEM((32 * 64, VH), F32),
            pltpu.VMEM((4, QTOK, WIDE), F32),
            pltpu.VMEM((4, QTOK, WIDE), F32),
            pltpu.VMEM((4, QTOK, WIDE), BF16),
            pltpu.VMEM((EXPERTS, ROWS, TOKENS), BF16),
            pltpu.VMEM((EXPERTS, TOKENS, ROWS), BF16),
            pltpu.VMEM((EXPERTS, TOKENS), F32),
            pltpu.VMEM((EXPERTS, TOKENS), F32),
            pltpu.VMEM((QTOK, COLS), F32),
            pltpu.VMEM((ROWS, 128), F32),
            pltpu.VMEM((XY, ROWS, WIDE), BF16),
            pltpu.VMEM((32, ROWS, WIDE), BF16),
            pltpu.VMEM((ROWS, UNITS), F32),
            pltpu.VMEM((ROWS, UNITS), F32),
            pltpu.VMEM((ROWS, 128), F32),
            pltpu.VMEM((ROWS, UNITS), BF16),
            pltpu.VMEM((XY, 2, ROWS, WIDE), BF16),
            pltpu.VMEM((XY, ROWS, WIDE), BF16),
            pltpu.VMEM((XY, ROWS, WIDE), BF16),
            pltpu.VMEM((XY, ROWS, WIDE), BF16),
            pltpu.VMEM((4, QTOK, WIDE), F32),
            pltpu.VMEM((4, QTOK, WIDE), F32),
            dma((6,)),
            dma((XY,)), dma((XY,)), dma((XY,)), dma((XY,)),
            dma((4,)), dma((4,)), dma((4,)), dma((4,)),
            dma((XY,)), dma((XY,)), dma((XY,)), dma((XY,)),
            dma((XY,)), dma((XY,)), dma((XY,)), dma((XY,)),
            dma((4,)), dma((4,)),
        ],
        compiler_params=pltpu.CompilerParams(
            collective_id=0, has_side_effects=True, vmem_limit_bytes=56 * 2**20
        ),
    )(
        query, new_latent, cache, cache_len, w_uv, w_out, hidden_in, norm_gain.reshape(1, COLS),
        routing, route_weight, w_gate_up, w_down,
    )


def solution(mesh):
    placed = (
        P("dp", "tp", None),
        P("dp", None),
        P("dp", None, None),
        P("dp"),
        P("tp", None, None),
        P("tp", "dp"),
        P("tp", "dp"),
        P("dp"),
        P(),
        P(),
        P(None, None, ("dp", "tp")),
        P(("dp", "tp"), None),
    )
    return jax.shard_map(
        on_device, mesh=mesh, in_specs=placed, out_specs=P("tp", "dp"), check_vma=False
    )
```

time: 244 us -> 75.1 us (0.31)
  the two profiles are of different devices: /device:TPU:1 before, /device:TPU:0 now
where the time goes in v1:
time: 75.1 us; the launch traced here: 74.8 us
  Pallas kernels  64.1 us (85%)
  local copies, waits for them, and re-layouts  10.7 us (14%)
    pallas_call x1, Pallas kernels, on_device(): pl.pallas_call(kernel, out_shape=jax.ShapeDtypeStruct((QTOK, COLS), BF16)...  64.1 us
    unnamed x5, local copies, waits for them, and re-layouts  10.7 us

profile of v1, /device:TPU:0, one launch (start us, length us, event | category | flops | bytes accessed | tf_op | source)
XLA Modules:
  0.0 74.8 jit_solution(11563124469559314545)
XLA Ops:
  0.0 1.4 %copy.15.routing = s32[128,8]{1,0:T(8,128)} copy(s32[128,8]{0,1:T(8,128)} %param.20) | data formatting | bytes 8192 | tf_op args[8]
  1.4 1.4 %copy.16.route_weight = f32[128,8]{1,0:T(8,128)} copy(f32[128,8]{0,1:T(8,128)} %param.21) | data formatting | bytes 8192 | tf_op args[9]
  2.8 2.2 %copy.14.w_out = bf16[2048,224]{1,0:T(8,128)(2,1)} copy(bf16[2048,224]{0,1:T(8,128)(2,1)} %param.17) | data formatting | bytes 1835008 | tf_op args[5]
  5.0 4.3 %copy.13.cache = bf16[2,1024,576]{2,1,0:T(8,128)(2,1)} copy(bf16[2,1024,576]{1,2,0:T(8,128)(2,1)} %param.14) | data formatting | bytes 4718592 | tf_op args[2]
  9.4 64.1 %shard_map.118 = bf16[32,224]{1,0:T(8,128)(2,1)} custom-call(bf16[4,16,576]{2,1,0:T(8,128)(2,1)} %query.1, bf16[4,576]{1,0:T(4,128)(2,1)} %new_latent.1, bf16[2,1024,576]{2,1,0:T(8,128)(2,1)} %copy.13.cache, s32[2]{0:T(128)} %cache_len.1, bf16[16,512,128]{2,1,0:T(8,128)(2,1)} %w_uv.1, bf16[2048,224]{1,0:T(8,128)(2,1)} %copy.14.w_out, ...), custom_call_target="tpu_custom_call" | custom-call | tf_op jit(solution)/shard_map/pallas_call | solution.py:352
  73.4 1.3 %copy.18 = bf16[32,224]{1,0:T(8,128)(2,1)} copy(bf16[32,224]{1,0:T(8,128)(2,1)} %shard_map.118) | data formatting | bytes 28672

commit v2 on v1

v2 whole, which is shorter than its diff:
```python
import jax
import jax.numpy as jnp
from jax import lax
from jax.experimental import pallas as pl
from jax.experimental.pallas import tpu as pltpu
from jax.sharding import PartitionSpec as P

D = 7168
LAT = 576
KVL = 512
ROPE = 64
VH = 128
MAXLEN = 1024
EXPERTS = 16
TOKENS = 128
TOP = 8
QTOK = 32
CAP = 24
ROWS = 4 * CAP
COLS = 224
WIDE = 256
UNITS = 256
XY = 16
HALF = D // 2
EPSILON = 1e-06
MESH = pl.DeviceIdType.MESH
F32 = jnp.float32
BF16 = jnp.bfloat16


def mm(a, b, dims=((1,), (0,)), precision=None):
    return lax.dot_general(a, b, (dims, ((), ())), preferred_element_type=F32, precision=precision)


OFFSETS = [(0, 0)] + sorted(
    [(a, b) for a in range(4) for b in range(4) if (a, b) != (0, 0)],
    key=lambda o: -(min(o[0], 4 - o[0]) + min(o[1], 4 - o[1])),
)


def kernel(
    query, new_latent, cache, cache_len, w_uv, w_out, hidden_in, gain, routing, route_weight,
    w_gate_up, w_down, out,
    cache_v, uv_v, out_v, gu_v, down_v,
    heads, heads32, part, part_in, hidden, pick, mem_t, pos_t, mid_s, wcol, merge,
    x_out, x_a, x_b, gate_s, up_s, sq_s, act_s, y_out, y_in,
    load_sem, hid_s, hid_r, w_s, w_r, a_s, a_r, a2_s, a2_r, c_s, c_r, e_s, e_r, e2_s, e2_r,
    f_s, f_r, g_s, g_r, g_own,
):
    dp = lax.axis_index("dp")
    z = lax.axis_index("tp")
    xy = dp // 2
    core = dp % 2
    sib = xy * 2 + (1 - core)
    side = dp // 16

    def peer(k):
        return (xy // 4 + OFFSETS[k][0]) % 4 * 4 + (xy + OFFSETS[k][1]) % 4

    def source(k):
        return (xy // 4 + 4 - OFFSETS[k][0]) % 4 * 4 + (xy + 4 - OFFSETS[k][1]) % 4

    def zpeer(j):
        return (z + j) % 4

    def remote(src, dst, send, recv, to_dp, to_z):
        return pltpu.make_async_remote_copy(
            src_ref=src, dst_ref=dst, send_sem=send, recv_sem=recv,
            device_id=(to_dp, to_z), device_id_type=MESH,
        )

    barrier = pltpu.get_barrier_semaphore()
    pl.semaphore_signal(barrier, inc=1, device_id=(sib, z), device_id_type=MESH)
    for k in range(1, XY):
        pl.semaphore_signal(barrier, inc=1, device_id=(peer(k) * 2 + core, z), device_id_type=MESH)
    for j in range(1, 4):
        pl.semaphore_signal(barrier, inc=1, device_id=(dp, zpeer(j)), device_id_type=MESH)

    half = pl.ds(pl.multiple_of(core * HALF, 128), HALF)
    other_half = pl.ds(pl.multiple_of((1 - core) * HALF, 128), HALF)
    loads = [
        pltpu.make_async_copy(cache.at[0], cache_v.at[0], load_sem.at[0]),
        pltpu.make_async_copy(cache.at[1], cache_v.at[1], load_sem.at[1]),
        pltpu.make_async_copy(w_uv, uv_v, load_sem.at[2]),
        pltpu.make_async_copy(w_out, out_v, load_sem.at[3]),
        pltpu.make_async_copy(w_gate_up, gu_v, load_sem.at[4]),
        pltpu.make_async_copy(w_down.at[:, half], down_v.at[core], load_sem.at[5]),
    ]
    for copy in loads:
        copy.start()
    hidden[z, :, :COLS] = hidden_in[...]
    hidden[z, :, COLS:] = jnp.zeros((QTOK, WIDE - COLS), BF16)

    scale = float(VH + ROPE) ** (-0.5)
    q_all = query[...].reshape(4 * XY, LAT)
    fresh = new_latent[...]
    near = mm(q_all, fresh, ((1,), (1,))) * scale
    row = lax.broadcasted_iota(jnp.int32, (64, 4), 0)
    col = lax.broadcasted_iota(jnp.int32, (64, 4), 1)
    near = jnp.where((row // 32 == col // 2) & (row // 16 >= col), near, -jnp.inf)
    contexts = []
    for b in range(2):
        loads[b].wait()
        q = q_all[32 * b : 32 * b + 32]
        far = mm(q, cache_v[b]) * scale
        place = lax.broadcasted_iota(jnp.int32, (32, MAXLEN), 1)
        far = jnp.where(place < cache_len[b], far, -jnp.inf)
        close = near[32 * b : 32 * b + 32]
        highest = jnp.maximum(
            jnp.max(far, axis=1, keepdims=True), jnp.max(close, axis=1, keepdims=True)
        )
        far = jnp.exp(far - highest)
        close = jnp.exp(close - highest)
        total = jnp.sum(far, axis=1, keepdims=True) + jnp.sum(close, axis=1, keepdims=True)
        context = mm((far / total).astype(BF16), cache_v[b, :KVL, :], ((1,), (1,)))
        context = context + mm((close / total).astype(BF16), fresh[:, :KVL])
        contexts.append(context.astype(BF16))
    context = jnp.concatenate(contexts, axis=0)
    loads[2].wait()
    row = lax.broadcasted_iota(jnp.int32, (64, VH), 0)
    head_out = jnp.zeros((64, VH), F32)
    for h in range(16):
        head_out = jnp.where(row % 16 == h, mm(context, uv_v[h]), head_out)
    heads[dp] = head_out.astype(BF16)

    pl.semaphore_wait(barrier, XY + 3)

    def a_copy(k):
        return remote(heads.at[dp], heads.at[dp], a_s, a_r.at[k], peer(k) * 2 + core, z)

    def a2_copy(k):
        which = source(k) * 2 + core
        return remote(heads.at[which], heads.at[which], a2_s, a2_r, sib, z)

    for k in range(1, XY):
        a_copy(k).start()
    a2_copy(0).start()

    def hid_copy(j):
        return remote(hidden.at[z], hidden.at[z], hid_s, hid_r, dp, zpeer(j))

    for j in range(1, 4):
        hid_copy(j).start()
    w_copy = remote(w_down.at[:, other_half], down_v.at[core], w_s, w_r, sib, z)
    w_copy.start()

    expert = lax.broadcasted_iota(jnp.int32, (EXPERTS, TOKENS), 0)
    member = jnp.zeros((EXPERTS, TOKENS), F32)
    share = jnp.zeros((1, TOKENS), F32)
    for k in range(TOP):
        named = routing[k : k + 1, :]
        member = member + jnp.where(named == expert, 1.0, 0.0)
        share = share + jnp.where(named == xy, route_weight[k : k + 1, :], 0.0)
    i0 = lax.broadcasted_iota(jnp.int32, (TOKENS, TOKENS), 0)
    i1 = lax.broadcasted_iota(jnp.int32, (TOKENS, TOKENS), 1)
    earlier = jnp.where((i0 < i1) & (i0 // QTOK == i1 // QTOK), 1.0, 0.0).astype(BF16)
    position = mm(member.astype(BF16), earlier)
    mem_t[...] = member
    pos_t[...] = position
    slot = lax.broadcasted_iota(jnp.int32, (ROWS, TOKENS), 0)
    token = lax.broadcasted_iota(jnp.int32, (ROWS, TOKENS), 1)
    in_block = slot // CAP == token // QTOK
    rank = (slot % CAP).astype(F32)
    for k in range(XY):
        e = pl.ds(peer(k), 1)
        here = (mem_t[e, :] > 0.5) & in_block & (pos_t[e, :] == rank)
        pick[k] = jnp.where(here, 1.0, 0.0).astype(BF16)
    weight = jnp.sum(pick[0].astype(F32) * share, axis=1, keepdims=True)
    wcol[...] = jnp.broadcast_to(weight, (ROWS, 128))
    i0 = lax.broadcasted_iota(jnp.int32, (TOKENS, QTOK), 0)
    i1 = lax.broadcasted_iota(jnp.int32, (TOKENS, QTOK), 1)
    own = jnp.where(i0 == i1 + z * QTOK, 1.0, 0.0).astype(BF16)
    spread_e = lax.broadcasted_iota(jnp.int32, (EXPERTS, EXPERTS * 2 * CAP), 0)
    spread_c = lax.broadcasted_iota(jnp.int32, (EXPERTS, EXPERTS * 2 * CAP), 1)
    spread = jnp.where(spread_c // (2 * CAP) == spread_e, 1.0, 0.0).astype(BF16)
    mem_own = mm(mm(member.astype(BF16), own).astype(BF16), spread, ((0,), (0,)))
    pos_own = mm(mm(position.astype(BF16), own).astype(BF16), spread, ((0,), (0,)))
    place = lax.broadcasted_iota(jnp.int32, (QTOK, EXPERTS * 2 * CAP), 1)
    found = (mem_own > 0.5) & (pos_own == (place % CAP).astype(F32))
    first = place % (2 * CAP) < CAP
    merge[:QTOK, :] = jnp.where(found & first, 1.0, 0.0).astype(BF16)
    merge[QTOK:, :] = jnp.where(found & (place % (2 * CAP) >= CAP), 1.0, 0.0).astype(BF16)

    for k in range(1, XY):
        a_copy(k).wait_recv()
        a2_copy(k).start()
    remote(heads.at[pl.ds(0, XY)], heads.at[pl.ds(0, XY)], a2_s, a2_r, sib, z).wait_recv()
    heads32[...] = heads[...].reshape(32 * 64, VH).astype(F32)
    loads[3].wait()
    projected = jnp.zeros((TOKENS, COLS), F32)
    for h in range(0, 16, 2):
        lhs = jnp.concatenate(
            [heads32[pl.ds(h, TOKENS, stride=16), :], heads32[pl.ds(h + 1, TOKENS, stride=16), :]], axis=1
        ).astype(BF16)
        projected = projected + mm(lhs, out_v[:, VH * h : VH * (h + 2)], ((1,), (1,)))
    part[:, :COLS] = projected.astype(BF16)
    part[:, COLS:] = jnp.zeros((TOKENS, WIDE - COLS), BF16)

    def c_copy(j):
        return remote(part, part_in.at[j], c_s, c_r.at[j], dp, zpeer(j))

    for j in range(1, 4):
        c_copy(j).start()
    remote(hidden.at[pl.ds(0, 3)], hidden.at[pl.ds(0, 3)], hid_s, hid_r, dp, zpeer(1)).wait_recv()
    mid = projected + hidden[...].reshape(TOKENS, WIDE)[:, :COLS].astype(F32)
    for j in (1, 3, 2):
        c_copy(j).wait_recv()
        mid = mid + part_in[j][:, :COLS].astype(F32)
    mid_s[...] = mid
    square = jnp.sum(mid * mid, axis=1, keepdims=True)
    square_hi = square.astype(BF16).astype(F32)
    square_lo = square - square_hi
    lane = lax.broadcasted_iota(jnp.int32, (TOKENS, WIDE - COLS), 1)
    spare = jnp.where(lane == 0, square_hi, jnp.where(lane == 1, square_lo, 0.0))
    all_rows = jnp.concatenate([(mid * gain[...]), spare], axis=1).astype(BF16)
    def e_copy(k):
        return remote(x_out.at[k], x_a.at[k], e_s, e_r.at[k], peer(k) * 2 + core, z)

    def e2_copy(k):
        return remote(x_a.at[k], x_b.at[k], e2_s, e2_r.at[k], sib, z)

    for first in range(1, XY, 5):
        rows = mm(pick[first : first + 5].reshape(5 * ROWS, TOKENS), all_rows).astype(BF16)
        for k in range(first, first + 5):
            x_out[k] = rows[ROWS * (k - first) : ROWS * (k - first + 1)]
            e_copy(k).start()
    x_a[0] = mm(pick[0], all_rows).astype(BF16)
    e2_copy(0).start()
    loads[4].wait()

    def take(buffer, ks, owner, start=False):
        gate, up, squares = (0.0, 0.0, 0.0) if start else (gate_s[...], up_s[...], sq_s[...])
        for k in ks:
            x = buffer[k]
            at = pl.ds(pl.multiple_of((source(k) * 2 + owner) * COLS, 32), COLS)
            gate = gate + mm(x[:, :COLS], gu_v[0, at, :])
            up = up + mm(x[:, :COLS], gu_v[1, at, :])
            squares = squares + x[:, 128:].astype(F32)
        gate_s[...] = gate
        up_s[...] = up
        sq_s[...] = squares

    def plane(ks):
        for k in ks:
            e_copy(k).wait_recv()
            e2_copy(k).start()

    def sibling(ks):
        for k in ks:
            e2_copy(k).wait_recv()

    take(x_a, [0], core, True)
    plane(range(1, 6))
    take(x_a, range(1, 6), core)
    plane(range(6, 11))
    sibling(range(0, 6))
    take(x_a, range(6, 11), core)
    take(x_b, range(0, 6), 1 - core)
    plane(range(11, 16))
    sibling(range(6, 11))
    take(x_b, range(6, 11), 1 - core)
    take(x_a, range(11, 16), core)
    sibling(range(11, 16))
    take(x_b, range(11, 16), 1 - core)
    square = sq_s[:, COLS - 128 : COLS - 127] + sq_s[:, COLS - 127 : COLS - 126]
    factor = lax.rsqrt(square / D + EPSILON)
    g = gate_s[...] * factor
    u = up_s[...] * factor
    act_s[core] = (g / (1.0 + jnp.exp(-g)) * u).astype(BF16)
    f_copy = remote(act_s.at[core], act_s.at[core], f_s, f_r, sib, z)
    f_copy.start()
    loads[5].wait()
    w_copy.wait_recv()
    f_copy.wait_recv()
    weight = wcol[:, :1]

    def g_copy(m, q):
        return remote(y_out.at[m, q], y_in.at[z * XY + xy], g_s, g_r, core * 16 + m, q)

    def g_self(m, q):
        return pltpu.make_async_copy(y_out.at[m, q], y_in.at[z * XY + xy], g_own)

    def results(n, _):
        group = (dp // 4 % 4 + n) % 4
        at = pl.ds(pl.multiple_of(group * 4 * COLS, 128), 4 * COLS)
        y = (mm(act_s[0], down_v[0, :, at]) + mm(act_s[1], down_v[1, :, at])) * weight
        for k in range(4):
            low = y[:, COLS * k : COLS * k + 128]
            high = jnp.concatenate(
                [y[:, COLS * k + 128 : COLS * (k + 1)], jnp.zeros((ROWS, WIDE - COLS), F32)], axis=1
            )
            m = group * 4 + k
            for q in range(4):
                at_q = slice(CAP * q, CAP * (q + 1))
                y_out[m, q] = jnp.concatenate([low[at_q], high[at_q]], axis=0).astype(BF16)
                to_self = (core * 16 + m == dp) & (z == q)

                @pl.when(to_self)
                def _():
                    g_self(m, q).start()

                @pl.when(jnp.logical_not(to_self))
                def _():
                    g_copy(m, q).start()

        return 0

    lax.fori_loop(0, 4, results, 0)
    mine = side == core

    def slabs(count):
        return remote(y_in.at[pl.ds(0, count)], y_in.at[pl.ds(0, count)], g_s, g_r, sib, z)

    @pl.when(mine)
    def _():
        slabs(63).wait_recv()
        g_self(0, 0).wait()

    @pl.when(jnp.logical_not(mine))
    def _():
        slabs(64).wait_recv()

    total = jnp.zeros((2 * QTOK, 128), F32)
    for j in range(4):
        total = total + mm(merge[...], y_in[XY * j : XY * (j + 1)].reshape(XY * 2 * CAP, 128))
    total = jnp.concatenate([total[:QTOK], total[QTOK:, : COLS - 128]], axis=1)
    out[...] = (mid_s[pl.ds(pl.multiple_of(z * QTOK, QTOK), QTOK), :] + total).astype(BF16)

    def left(ref, sem):
        remote(ref, ref, sem, w_r, sib, z).wait_send()

    left(heads.at[pl.ds(0, 15)], a_s)
    left(heads.at[pl.ds(0, 16)], a2_s)
    left(hidden.at[pl.ds(0, 3)], hid_s)
    w_copy.wait_send()
    left(part_in.at[pl.ds(0, 3)], c_s)
    left(x_out.at[pl.ds(0, 15)], e_s)
    left(x_a, e2_s)
    f_copy.wait_send()

    @pl.when(mine)
    def _():
        slabs(63).wait_send()

    @pl.when(jnp.logical_not(mine))
    def _():
        slabs(64).wait_send()


def on_device(
    query, new_latent, cache, cache_len, w_uv, w_out, hidden_in, norm_gain, routing, route_weight,
    w_gate_up, w_down,
):
    vmem = pl.BlockSpec(memory_space=pltpu.VMEM)
    smem = pl.BlockSpec(memory_space=pltpu.SMEM)
    hbm = pl.BlockSpec(memory_space=pl.ANY)
    dma = pltpu.SemaphoreType.DMA
    return pl.pallas_call(
        kernel,
        out_shape=jax.ShapeDtypeStruct((QTOK, COLS), BF16),
        in_specs=[vmem, vmem, hbm, smem, hbm, hbm, vmem, vmem, vmem, vmem, hbm, hbm],
        out_specs=vmem,
        scratch_shapes=[
            pltpu.VMEM((2, LAT, MAXLEN), BF16),
            pltpu.VMEM((16, KVL, VH), BF16),
            pltpu.VMEM((COLS, 16 * VH), BF16),
            pltpu.VMEM((2, D, UNITS), BF16),
            pltpu.VMEM((2, UNITS, HALF), BF16),
            pltpu.VMEM((32, 64, VH), BF16),
            pltpu.VMEM((32 * 64, VH), F32),
            pltpu.VMEM((TOKENS, WIDE), BF16),
            pltpu.VMEM((4, TOKENS, WIDE), BF16),
            pltpu.VMEM((4, QTOK, WIDE), BF16),
            pltpu.VMEM((XY, ROWS, TOKENS), BF16),
            pltpu.VMEM((EXPERTS, TOKENS), F32),
            pltpu.VMEM((EXPERTS, TOKENS), F32),
            pltpu.VMEM((TOKENS, COLS), F32),
            pltpu.VMEM((ROWS, 128), F32),
            pltpu.VMEM((2 * QTOK, XY * 2 * CAP), BF16),
            pltpu.VMEM((XY, ROWS, WIDE), BF16),
            pltpu.VMEM((XY, ROWS, WIDE), BF16),
            pltpu.VMEM((XY, ROWS, WIDE), BF16),
            pltpu.VMEM((ROWS, UNITS), F32),
            pltpu.VMEM((ROWS, UNITS), F32),
            pltpu.VMEM((ROWS, 128), F32),
            pltpu.VMEM((2, ROWS, UNITS), BF16),
            pltpu.VMEM((XY, 4, 2 * CAP, 128), BF16),
            pltpu.VMEM((4 * XY, 2 * CAP, 128), BF16),
            dma((6,)),
            dma, dma, dma, dma,
            dma, dma((XY,)), dma, dma,
            dma, dma((4,)),
            dma, dma((XY,)), dma, dma((XY,)),
            dma, dma, dma, dma, dma,
        ],
        compiler_params=pltpu.CompilerParams(
            collective_id=0, has_side_effects=True, vmem_limit_bytes=56 * 2**20
        ),
    )(
        query, new_latent, cache.transpose(0, 2, 1), cache_len, w_uv, w_out.T, hidden_in,
        norm_gain.reshape(1, COLS), routing.T, route_weight.T, w_gate_up, w_down,
    )


def solution(mesh):
    placed = (
        P("dp", "tp", None),
        P("dp", None),
        P("dp", None, None),
        P("dp"),
        P("tp", None, None),
        P("tp", "dp"),
        P("tp", "dp"),
        P("dp"),
        P(),
        P(),
        P(None, None, ("dp", "tp")),
        P(("dp", "tp"), None),
    )
    return jax.shard_map(
        on_device, mesh=mesh, in_specs=placed, out_specs=P("tp", "dp"), check_vma=False
    )
```

time: 75.1 us -> 55.6 us (0.74)
  the two profiles are of different devices: /device:TPU:0 before, /device:TPU:1 now
where the time goes in v2:
time: 55.6 us; the launch traced here: 55.5 us
  Pallas kernels  54.1 us (97%)
  local copies, waits for them, and re-layouts  1.32 us (2%)
    pallas_call x1, Pallas kernels, on_device(): pl.pallas_call(kernel, out_shape=jax.ShapeDtypeStruct((QTOK, COLS), BF16)...  54.1 us
    unnamed x1, local copies, waits for them, and re-layouts  1.32 us

profile of v2, /device:TPU:1, one launch (start us, length us, event | category | flops | bytes accessed | tf_op | source)
XLA Modules:
  0.0 55.5 jit_solution(18408347351120763177)
XLA Ops:
  0.0 54.1 %shard_map.118 = bf16[32,224]{1,0:T(8,128)(2,1)} custom-call(bf16[4,16,576]{2,1,0:T(8,128)(2,1)} %query.1, bf16[4,576]{1,0:T(4,128)(2,1)} %new_latent.1, bf16[2,576,1024]{2,1,0:T(8,128)(2,1)} %bitcast.5, s32[2]{0:T(128)} %cache_len.1, bf16[16,512,128]{2,1,0:T(8,128)(2,1)} %w_uv.1, bf16[224,2048]{1,0:T(8,128)(2,1)} %bitcast.6, bf16[32,224]{1,0:T(8,128)(2,1)} %hidden_in.1, ...), custom_call_target="tpu_custom_call" | custom-call | tf_op jit(solution)/shard_map/pallas_call | solution.py:358
  54.1 1.3 %copy.14 = bf16[32,224]{1,0:T(8,128)(2,1)} copy(bf16[32,224]{1,0:T(8,128)(2,1)} %shard_map.118) | data formatting | bytes 28672

commit v3 on v2

--- a/solution.py
+++ b/solution.py
@@ -22,6 +22,7 @@
 UNITS = 256
 XY = 16
 HALF = D // 2
+PART = ROWS // 2
 EPSILON = 1e-06
 MESH = pl.DeviceIdType.MESH
 F32 = jnp.float32
@@ -42,8 +43,8 @@
     query, new_latent, cache, cache_len, w_uv, w_out, hidden_in, gain, routing, route_weight,
     w_gate_up, w_down, out,
     cache_v, uv_v, out_v, gu_v, down_v,
-    heads, heads32, part, part_in, hidden, pick, mem_t, pos_t, mid_s, wcol, merge,
-    x_out, x_a, x_b, gate_s, up_s, sq_s, act_s, y_out, y_in,
+    heads_a, heads_b, heads32, part, part_in, hidden, pick, mem_t, pos_t, mid_s, wcol, merge,
+    x_out, x_a, x_b, act_s, y_out, y_in,
     load_sem, hid_s, hid_r, w_s, w_r, a_s, a_r, a2_s, a2_r, c_s, c_r, e_s, e_r, e2_s, e2_r,
     f_s, f_r, g_s, g_r, g_own,
 ):
@@ -121,20 +122,19 @@
     head_out = jnp.zeros((64, VH), F32)
     for h in range(16):
         head_out = jnp.where(row % 16 == h, mm(context, uv_v[h]), head_out)
-    heads[dp] = head_out.astype(BF16)
+    heads_a[0] = head_out.astype(BF16)
 
     pl.semaphore_wait(barrier, XY + 3)
 
     def a_copy(k):
-        return remote(heads.at[dp], heads.at[dp], a_s, a_r.at[k], peer(k) * 2 + core, z)
-
-    def a2_copy(k):
-        which = source(k) * 2 + core
-        return remote(heads.at[which], heads.at[which], a2_s, a2_r, sib, z)
+        return remote(heads_a.at[0], heads_a.at[k], a_s, a_r.at[(k - 1) // 5], peer(k) * 2 + core, z)
+
+    def a2_copy(ks, sem):
+        return remote(heads_a.at[ks], heads_b.at[ks], a2_s, sem, sib, z)
 
     for k in range(1, XY):
         a_copy(k).start()
-    a2_copy(0).start()
+    a2_copy(pl.ds(0, 1), a2_r.at[3]).start()
 
     def hid_copy(j):
         return remote(hidden.at[z], hidden.at[z], hid_s, hid_r, dp, zpeer(j))
@@ -164,9 +164,11 @@
     for k in range(XY):
         e = pl.ds(peer(k), 1)
         here = (mem_t[e, :] > 0.5) & in_block & (pos_t[e, :] == rank)
-        pick[k] = jnp.where(here, 1.0, 0.0).astype(BF16)
-    weight = jnp.sum(pick[0].astype(F32) * share, axis=1, keepdims=True)
-    wcol[...] = jnp.broadcast_to(weight, (ROWS, 128))
+        chosen = jnp.where(here, 1.0, 0.0)
+        for h in range(2):
+            pick[h, k] = chosen[h * PART : (h + 1) * PART].astype(BF16)
+        if k == 0:
+            wcol[...] = jnp.broadcast_to(jnp.sum(chosen * share, axis=1, keepdims=True), (ROWS, 128))
     i0 = lax.broadcasted_iota(jnp.int32, (TOKENS, QTOK), 0)
     i1 = lax.broadcasted_iota(jnp.int32, (TOKENS, QTOK), 1)
     own = jnp.where(i0 == i1 + z * QTOK, 1.0, 0.0).astype(BF16)
@@ -181,11 +183,26 @@
     merge[:QTOK, :] = jnp.where(found & first, 1.0, 0.0).astype(BF16)
     merge[QTOK:, :] = jnp.where(found & (place % (2 * CAP) >= CAP), 1.0, 0.0).astype(BF16)
 
-    for k in range(1, XY):
-        a_copy(k).wait_recv()
-        a2_copy(k).start()
-    remote(heads.at[pl.ds(0, XY)], heads.at[pl.ds(0, XY)], a2_s, a2_r, sib, z).wait_recv()
-    heads32[...] = heads[...].reshape(32 * 64, VH).astype(F32)
+    def groups(buffer, sem):
+        return remote(buffer, buffer, a_s, sem, sib, z)
+
+    fives = [pl.ds(5 * g + 1, 5) for g in range(3)]
+
+    def spread_heads(buffer, owner, ks):
+        for k in ks:
+            at = pl.multiple_of((source(k) * 2 + owner) * 64, 64)
+            heads32[pl.ds(at, 64), :] = buffer[k].astype(F32)
+
+    spread_heads(heads_a, core, [0])
+    for g in range(3):
+        groups(heads_a.at[fives[g]], a_r.at[g]).wait_recv()
+        a2_copy(fives[g], a2_r.at[g]).start()
+        spread_heads(heads_a, core, range(5 * g + 1, 5 * g + 6))
+    a2_copy(pl.ds(0, 1), a2_r.at[3]).wait_recv()
+    spread_heads(heads_b, 1 - core, [0])
+    for g in range(3):
+        a2_copy(fives[g], a2_r.at[g]).wait_recv()
+        spread_heads(heads_b, 1 - core, range(5 * g + 1, 5 * g + 6))
     loads[3].wait()
     projected = jnp.zeros((TOKENS, COLS), F32)
     for h in range(0, 16, 2):
@@ -213,66 +230,62 @@
     lane = lax.broadcasted_iota(jnp.int32, (TOKENS, WIDE - COLS), 1)
     spare = jnp.where(lane == 0, square_hi, jnp.where(lane == 1, square_lo, 0.0))
     all_rows = jnp.concatenate([(mid * gain[...]), spare], axis=1).astype(BF16)
-    def e_copy(k):
-        return remote(x_out.at[k], x_a.at[k], e_s, e_r.at[k], peer(k) * 2 + core, z)
-
-    def e2_copy(k):
-        return remote(x_a.at[k], x_b.at[k], e2_s, e2_r.at[k], sib, z)
-
-    for first in range(1, XY, 5):
-        rows = mm(pick[first : first + 5].reshape(5 * ROWS, TOKENS), all_rows).astype(BF16)
-        for k in range(first, first + 5):
-            x_out[k] = rows[ROWS * (k - first) : ROWS * (k - first + 1)]
-            e_copy(k).start()
-    x_a[0] = mm(pick[0], all_rows).astype(BF16)
-    e2_copy(0).start()
+    def e_copy(h, k):
+        return remote(
+            x_out.at[h, k], x_a.at[h, k], e_s, e_r.at[h * 3 + (k - 1) // 5], peer(k) * 2 + core, z
+        )
+
+    def e2_copy(h, ks, n):
+        return remote(x_a.at[h, ks], x_b.at[h, ks], e2_s, e2_r.at[h * 4 + n], sib, z)
+
+    for h in range(2):
+        for first in range(1, XY, 5):
+            rows = mm(pick[h, first : first + 5].reshape(5 * PART, TOKENS), all_rows).astype(BF16)
+            for k in range(first, first + 5):
+                x_out[h, k] = rows[PART * (k - first) : PART * (k - first + 1)]
+                e_copy(h, k).start()
+        x_a[h, 0] = mm(pick[h, 0], all_rows).astype(BF16)
+        e2_copy(h, pl.ds(0, 1), 3).start()
     loads[4].wait()
 
-    def take(buffer, ks, owner, start=False):
-        gate, up, squares = (0.0, 0.0, 0.0) if start else (gate_s[...], up_s[...], sq_s[...])
+    def take(sums, buffer, h, ks, owner):
+        gate, up, squares = sums
         for k in ks:
-            x = buffer[k]
+            x = buffer[h, k]
             at = pl.ds(pl.multiple_of((source(k) * 2 + owner) * COLS, 32), COLS)
             gate = gate + mm(x[:, :COLS], gu_v[0, at, :])
             up = up + mm(x[:, :COLS], gu_v[1, at, :])
             squares = squares + x[:, 128:].astype(F32)
-        gate_s[...] = gate
-        up_s[...] = up
-        sq_s[...] = squares
-
-    def plane(ks):
-        for k in ks:
-            e_copy(k).wait_recv()
-            e2_copy(k).start()
-
-    def sibling(ks):
-        for k in ks:
-            e2_copy(k).wait_recv()
-
-    take(x_a, [0], core, True)
-    plane(range(1, 6))
-    take(x_a, range(1, 6), core)
-    plane(range(6, 11))
-    sibling(range(0, 6))
-    take(x_a, range(6, 11), core)
-    take(x_b, range(0, 6), 1 - core)
-    plane(range(11, 16))
-    sibling(range(6, 11))
-    take(x_b, range(6, 11), 1 - core)
-    take(x_a, range(11, 16), core)
-    sibling(range(11, 16))
-    take(x_b, range(11, 16), 1 - core)
-    square = sq_s[:, COLS - 128 : COLS - 127] + sq_s[:, COLS - 127 : COLS - 126]
-    factor = lax.rsqrt(square / D + EPSILON)
-    g = gate_s[...] * factor
-    u = up_s[...] * factor
-    act_s[core] = (g / (1.0 + jnp.exp(-g)) * u).astype(BF16)
-    f_copy = remote(act_s.at[core], act_s.at[core], f_s, f_r, sib, z)
-    f_copy.start()
-    loads[5].wait()
-    w_copy.wait_recv()
-    f_copy.wait_recv()
-    weight = wcol[:, :1]
+        return gate, up, squares
+
+    def arrive(h, g):
+        groups(x_a.at[h, fives[g]], e_r.at[h * 3 + g]).wait_recv()
+        e2_copy(h, fives[g], g).start()
+
+    def take_a(sums, h, g):
+        return take(sums, x_a, h, range(5 * g + 1, 5 * g + 6), core)
+
+    def take_b(sums, h, g):
+        e2_copy(h, fives[g], g).wait_recv()
+        return take(sums, x_b, h, range(5 * g + 1, 5 * g + 6), 1 - core)
+
+    def take_own(h):
+        sums = (jnp.zeros((PART, UNITS), F32), jnp.zeros((PART, UNITS), F32), jnp.zeros((PART, 128), F32))
+        sums = take(sums, x_a, h, [0], core)
+        e2_copy(h, pl.ds(0, 1), 3).wait_recv()
+        return take(sums, x_b, h, [0], 1 - core)
+
+    def f_copy(h):
+        return remote(act_s.at[core, h], act_s.at[core, h], f_s.at[h], f_r.at[h], sib, z)
+
+    def activate(sums, h):
+        gate, up, squares = sums
+        square = squares[:, COLS - 128 : COLS - 127] + squares[:, COLS - 127 : COLS - 126]
+        factor = lax.rsqrt(square / D + EPSILON)
+        g = gate * factor
+        u = up * factor
+        act_s[core, h] = (g / (1.0 + jnp.exp(-g)) * u).astype(BF16)
+        f_copy(h).start()
 
     def g_copy(m, q):
         return remote(y_out.at[m, q], y_in.at[z * XY + xy], g_s, g_r, core * 16 + m, q)
@@ -280,32 +293,66 @@
     def g_self(m, q):
         return pltpu.make_async_copy(y_out.at[m, q], y_in.at[z * XY + xy], g_own)
 
-    def results(n, _):
+    def results(h, n):
         group = (dp // 4 % 4 + n) % 4
         at = pl.ds(pl.multiple_of(group * 4 * COLS, 128), 4 * COLS)
-        y = (mm(act_s[0], down_v[0, :, at]) + mm(act_s[1], down_v[1, :, at])) * weight
+        y = mm(act_s[0, h], down_v[0, :, at]) + mm(act_s[1, h], down_v[1, :, at])
+        y = y * wcol[PART * h : PART * (h + 1), :1]
         for k in range(4):
             low = y[:, COLS * k : COLS * k + 128]
             high = jnp.concatenate(
-                [y[:, COLS * k + 128 : COLS * (k + 1)], jnp.zeros((ROWS, WIDE - COLS), F32)], axis=1
+                [y[:, COLS * k + 128 : COLS * (k + 1)], jnp.zeros((PART, WIDE - COLS), F32)], axis=1
             )
-            m = group * 4 + k
-            for q in range(4):
+            for q in range(2):
                 at_q = slice(CAP * q, CAP * (q + 1))
-                y_out[m, q] = jnp.concatenate([low[at_q], high[at_q]], axis=0).astype(BF16)
-                to_self = (core * 16 + m == dp) & (z == q)
-
-                @pl.when(to_self)
-                def _():
-                    g_self(m, q).start()
-
-                @pl.when(jnp.logical_not(to_self))
-                def _():
+                slab = jnp.concatenate([low[at_q], high[at_q]], axis=0)
+                y_out[group * 4 + k, 2 * h + q] = slab.astype(BF16)
+        for i in range(4):
+            for j in range(2):
+                m = group * 4 + (dp + i) % 4
+                q = 2 * h + (z + j) % 2
+                if n == 0 and i == 0 and j == 0:
+                    to_self = (core * 16 + m == dp) & (z == q)
+
+                    @pl.when(to_self)
+                    def _():
+                        g_self(m, q).start()
+
+                    @pl.when(jnp.logical_not(to_self))
+                    def _():
+                        g_copy(m, q).start()
+
+                else:
                     g_copy(m, q).start()
 
-        return 0
-
-    lax.fori_loop(0, 4, results, 0)
+    sums = take_own(0)
+    for g in range(3):
+        arrive(0, g)
+        sums = take_a(sums, 0, g)
+    for g in range(3):
+        sums = take_b(sums, 0, g)
+    activate(sums, 0)
+    sums = take_own(1)
+    arrive(1, 0)
+    sums = take_a(sums, 1, 0)
+    sums = take_b(sums, 1, 0)
+    loads[5].wait()
+    w_copy.wait_recv()
+    f_copy(0).wait_recv()
+    results(0, 0)
+    arrive(1, 1)
+    results(0, 1)
+    results(0, 2)
+    arrive(1, 2)
+    results(0, 3)
+    sums = take_a(sums, 1, 1)
+    sums = take_b(sums, 1, 1)
+    sums = take_a(sums, 1, 2)
+    sums = take_b(sums, 1, 2)
+    activate(sums, 1)
+    f_copy(1).wait_recv()
+    for n in range(4):
+        results(1, n)
     mine = side == core
 
     def slabs(count):
@@ -329,14 +376,16 @@
     def left(ref, sem):
         remote(ref, ref, sem, w_r, sib, z).wait_send()
 
-    left(heads.at[pl.ds(0, 15)], a_s)
-    left(heads.at[pl.ds(0, 16)], a2_s)
+    left(heads_a.at[pl.ds(0, 15)], a_s)
+    left(heads_a, a2_s)
     left(hidden.at[pl.ds(0, 3)], hid_s)
     w_copy.wait_send()
     left(part_in.at[pl.ds(0, 3)], c_s)
-    left(x_out.at[pl.ds(0, 15)], e_s)
+    left(x_out.at[0], e_s)
+    left(x_out.at[0, pl.ds(0, 14)], e_s)
     left(x_a, e2_s)
-    f_copy.wait_send()
+    for h in range(2):
+        f_copy(h).wait_send()
 
     @pl.when(mine)
     def _():
@@ -366,32 +415,30 @@
             pltpu.VMEM((COLS, 16 * VH), BF16),
             pltpu.VMEM((2, D, UNITS), BF16),
             pltpu.VMEM((2, UNITS, HALF), BF16),
-            pltpu.VMEM((32, 64, VH), BF16),
+            pltpu.VMEM((XY, 64, VH), BF16),
+            pltpu.VMEM((XY, 64, VH), BF16),
             pltpu.VMEM((32 * 64, VH), F32),
             pltpu.VMEM((TOKENS, WIDE), BF16),
             pltpu.VMEM((4, TOKENS, WIDE), BF16),
             pltpu.VMEM((4, QTOK, WIDE), BF16),
-            pltpu.VMEM((XY, ROWS, TOKENS), BF16),
+            pltpu.VMEM((2, XY, PART, TOKENS), BF16),
             pltpu.VMEM((EXPERTS, TOKENS), F32),
             pltpu.VMEM((EXPERTS, TOKENS), F32),
             pltpu.VMEM((TOKENS, COLS), F32),
             pltpu.VMEM((ROWS, 128), F32),
             pltpu.VMEM((2 * QTOK, XY * 2 * CAP), BF16),
-            pltpu.VMEM((XY, ROWS, WIDE), BF16),
-            pltpu.VMEM((XY, ROWS, WIDE), BF16),
-            pltpu.VMEM((XY, ROWS, WIDE), BF16),
-            pltpu.VMEM((ROWS, UNITS), F32),
-            pltpu.VMEM((ROWS, UNITS), F32),
-            pltpu.VMEM((ROWS, 128), F32),
-            pltpu.VMEM((2, ROWS, UNITS), BF16),
+            pltpu.VMEM((2, XY, PART, WIDE), BF16),
+            pltpu.VMEM((2, XY, PART, WIDE), BF16),
+            pltpu.VMEM((2, XY, PART, WIDE), BF16),
+            pltpu.VMEM((2, 2, PART, UNITS), BF16),
             pltpu.VMEM((XY, 4, 2 * CAP, 128), BF16),
             pltpu.VMEM((4 * XY, 2 * CAP, 128), BF16),
             dma((6,)),
             dma, dma, dma, dma,
-            dma, dma((XY,)), dma, dma,
+            dma, dma((3,)), dma, dma((4,)),
             dma, dma((4,)),
-            dma, dma((XY,)), dma, dma((XY,)),
-            dma, dma, dma, dma, dma,
+            dma, dma((6,)), dma, dma((8,)),
+            dma((2,)), dma((2,)), dma, dma, dma,
         ],
         compiler_params=pltpu.CompilerParams(
             collective_id=0, has_side_effects=True, vmem_limit_bytes=56 * 2**20

time: 55.6 us -> 51.6 us (0.928); the launches traced: 55.5 us -> 50.7 us
  Pallas kernels: 54.1 us -> 49.3 us
    pallas_call x1, Pallas kernels: 54.1 us -> 49.3 us  [on_device(): pl.pallas_call(kernel, out_shape=jax.ShapeDtypeStruct((QTOK, COLS), BF16)...]
where the time goes in v3:
time: 51.6 us; the launch traced here: 50.7 us
  Pallas kernels  49.3 us (96%)
  local copies, waits for them, and re-layouts  1.32 us (3%)
    pallas_call x1, Pallas kernels, on_device(): pl.pallas_call(kernel, out_shape=jax.ShapeDtypeStruct((QTOK, COLS), BF16)...  49.3 us
    unnamed x1, local copies, waits for them, and re-layouts  1.32 us

profile of v3, /device:TPU:1, one launch (start us, length us, event | category | flops | bytes accessed | tf_op | source)
XLA Modules:
  0.0 50.7 jit_solution(14423862205564310430)
XLA Ops:
  0.0 49.3 %shard_map.118 = bf16[32,224]{1,0:T(8,128)(2,1)} custom-call(bf16[4,16,576]{2,1,0:T(8,128)(2,1)} %query.1, bf16[4,576]{1,0:T(4,128)(2,1)} %new_latent.1, bf16[2,576,1024]{2,1,0:T(8,128)(2,1)} %bitcast.5, s32[2]{0:T(128)} %cache_len.1, bf16[16,512,128]{2,1,0:T(8,128)(2,1)} %w_uv.1, bf16[224,2048]{1,0:T(8,128)(2,1)} %bitcast.6, bf16[32,224]{1,0:T(8,128)(2,1)} %hidden_in.1, ...), custom_call_target="tpu_custom_call" | custom-call | tf_op jit(solution)/shard_map/pallas_call | solution.py:407
  49.3 1.3 %copy.14 = bf16[32,224]{1,0:T(8,128)(2,1)} copy(bf16[32,224]{1,0:T(8,128)(2,1)} %shard_map.118) | data formatting | bytes 28672

commit v4 on v3

--- a/solution.py
+++ b/solution.py
@@ -40,10 +40,10 @@
 
 
 def kernel(
-    query, new_latent, cache, cache_len, w_uv, w_out, hidden_in, gain, routing, route_weight,
-    w_gate_up, w_down, out,
-    cache_v, uv_v, out_v, gu_v, down_v,
-    heads_a, heads_b, heads32, part, part_in, hidden, pick, mem_t, pos_t, mid_s, wcol, merge,
+    query_h, new_latent_h, cache, cache_len_h, w_uv, w_out, hidden_in_h, gain_h, routing_h,
+    route_weight_h, w_gate_up, w_down, out,
+    query, new_latent, cache_len, hidden_in, gain, routing, route_weight, cache_v, uv_v, out_v, gu_v, down_v, down_p,
+    heads_a, heads_b, heads32, proj, part, part_in, hidden, pick, mem_t, pos_t, mid_s, wcol, merge,
     x_out, x_a, x_b, act_s, y_out, y_in,
     load_sem, hid_s, hid_r, w_s, w_r, a_s, a_r, a2_s, a2_r, c_s, c_r, e_s, e_r, e2_s, e2_r,
     f_s, f_r, g_s, g_r, g_own,
@@ -71,11 +71,11 @@
         )
 
     barrier = pltpu.get_barrier_semaphore()
-    pl.semaphore_signal(barrier, inc=1, device_id=(sib, z), device_id_type=MESH)
     for k in range(1, XY):
         pl.semaphore_signal(barrier, inc=1, device_id=(peer(k) * 2 + core, z), device_id_type=MESH)
-    for j in range(1, 4):
+    for j in (2, 1, 3):
         pl.semaphore_signal(barrier, inc=1, device_id=(dp, zpeer(j)), device_id_type=MESH)
+    pl.semaphore_signal(barrier, inc=1, device_id=(sib, z), device_id_type=MESH)
 
     half = pl.ds(pl.multiple_of(core * HALF, 128), HALF)
     other_half = pl.ds(pl.multiple_of((1 - core) * HALF, 128), HALF)
@@ -87,10 +87,17 @@
         pltpu.make_async_copy(w_gate_up, gu_v, load_sem.at[4]),
         pltpu.make_async_copy(w_down.at[:, half], down_v.at[core], load_sem.at[5]),
     ]
-    for copy in loads:
+    small = [
+        pltpu.make_async_copy(src, dst, load_sem.at[6 + n])
+        for n, (src, dst) in enumerate([
+            (query_h, query), (new_latent_h, new_latent), (cache_len_h, cache_len), (hidden_in_h, hidden_in),
+            (gain_h, gain), (routing_h, routing), (route_weight_h, route_weight),
+        ])
+    ]
+    for copy in small[:3] + loads[:3] + small[3:] + loads[3:]:
         copy.start()
-    hidden[z, :, :COLS] = hidden_in[...]
-    hidden[z, :, COLS:] = jnp.zeros((QTOK, WIDE - COLS), BF16)
+    for copy in small[:3]:
+        copy.wait()
 
     scale = float(VH + ROPE) ** (-0.5)
     q_all = query[...].reshape(4 * XY, LAT)
@@ -124,6 +131,10 @@
         head_out = jnp.where(row % 16 == h, mm(context, uv_v[h]), head_out)
     heads_a[0] = head_out.astype(BF16)
 
+    for copy in small[3:]:
+        copy.wait()
+    hidden[z, :, :COLS] = hidden_in[...]
+    hidden[z, :, COLS:] = jnp.zeros((QTOK, WIDE - COLS), BF16)
     pl.semaphore_wait(barrier, XY + 3)
 
     def a_copy(k):
@@ -147,10 +158,13 @@
     expert = lax.broadcasted_iota(jnp.int32, (EXPERTS, TOKENS), 0)
     member = jnp.zeros((EXPERTS, TOKENS), F32)
     share = jnp.zeros((1, TOKENS), F32)
+    turn = (3 - z) * QTOK
+    turned = pltpu.roll(routing[...], turn, 1)
+    turned_weight = pltpu.roll(route_weight[...], turn, 1)
     for k in range(TOP):
-        named = routing[k : k + 1, :]
+        named = turned[k : k + 1, :]
         member = member + jnp.where(named == expert, 1.0, 0.0)
-        share = share + jnp.where(named == xy, route_weight[k : k + 1, :], 0.0)
+        share = share + jnp.where(named == xy, turned_weight[k : k + 1, :], 0.0)
     i0 = lax.broadcasted_iota(jnp.int32, (TOKENS, TOKENS), 0)
     i1 = lax.broadcasted_iota(jnp.int32, (TOKENS, TOKENS), 1)
     earlier = jnp.where((i0 < i1) & (i0 // QTOK == i1 // QTOK), 1.0, 0.0).astype(BF16)
@@ -166,12 +180,12 @@
         here = (mem_t[e, :] > 0.5) & in_block & (pos_t[e, :] == rank)
         chosen = jnp.where(here, 1.0, 0.0)
         for h in range(2):
-            pick[h, k] = chosen[h * PART : (h + 1) * PART].astype(BF16)
+            pick[h, k] = chosen[h * PART : (h + 1) * PART, h * 2 * QTOK : (h + 1) * 2 * QTOK].astype(BF16)
         if k == 0:
             wcol[...] = jnp.broadcast_to(jnp.sum(chosen * share, axis=1, keepdims=True), (ROWS, 128))
     i0 = lax.broadcasted_iota(jnp.int32, (TOKENS, QTOK), 0)
     i1 = lax.broadcasted_iota(jnp.int32, (TOKENS, QTOK), 1)
-    own = jnp.where(i0 == i1 + z * QTOK, 1.0, 0.0).astype(BF16)
+    own = jnp.where(i0 == i1 + 3 * QTOK, 1.0, 0.0).astype(BF16)
     spread_e = lax.broadcasted_iota(jnp.int32, (EXPERTS, EXPERTS * 2 * CAP), 0)
     spread_c = lax.broadcasted_iota(jnp.int32, (EXPERTS, EXPERTS * 2 * CAP), 1)
     spread = jnp.where(spread_c // (2 * CAP) == spread_e, 1.0, 0.0).astype(BF16)
@@ -183,6 +197,16 @@
     merge[:QTOK, :] = jnp.where(found & first, 1.0, 0.0).astype(BF16)
     merge[QTOK:, :] = jnp.where(found & (place % (2 * CAP) >= CAP), 1.0, 0.0).astype(BF16)
 
+    def spread_down(which):
+        for m in range(16):
+            first, last = COLS * m // 128, (COLS * (m + 1) + 127) // 128
+            at = COLS * m - 128 * first
+            piece = down_v[which, :, 128 * first : 128 * last][:, at : at + COLS]
+            down_p[which, m, :, :COLS] = piece
+            down_p[which, m, :, COLS:] = jnp.zeros((UNITS, WIDE - COLS), BF16)
+
+    loads[5].wait()
+    spread_down(core)
     def groups(buffer, sem):
         return remote(buffer, buffer, a_s, sem, sib, z)
 
@@ -210,26 +234,39 @@
             [heads32[pl.ds(h, TOKENS, stride=16), :], heads32[pl.ds(h + 1, TOKENS, stride=16), :]], axis=1
         ).astype(BF16)
         projected = projected + mm(lhs, out_v[:, VH * h : VH * (h + 2)], ((1,), (1,)))
-    part[:, :COLS] = projected.astype(BF16)
-    part[:, COLS:] = jnp.zeros((TOKENS, WIDE - COLS), BF16)
-
-    def c_copy(j):
-        return remote(part, part_in.at[j], c_s, c_r.at[j], dp, zpeer(j))
-
-    for j in range(1, 4):
-        c_copy(j).start()
+    for q in range(5):
+        block = projected[QTOK * (q % 4) : QTOK * (q % 4 + 1)]
+        part[q, :, :COLS] = block.astype(BF16)
+        part[q, :, COLS:] = jnp.zeros((QTOK, WIDE - COLS), BF16)
+        if q < 4:
+            proj[q] = block
+
+    def c_copy(h, j):
+        blocks = part.at[pl.ds((z + j + 1 + 2 * h) % 4, 2)]
+        return remote(blocks, part_in.at[h, j], c_s, c_r.at[h * 4 + j], dp, zpeer(j))
+
+    for h in range(2):
+        for j in (2, 1, 3):
+            c_copy(h, j).start()
+    w_copy.wait_recv()
+    spread_down(1 - core)
     remote(hidden.at[pl.ds(0, 3)], hidden.at[pl.ds(0, 3)], hid_s, hid_r, dp, zpeer(1)).wait_recv()
-    mid = projected + hidden[...].reshape(TOKENS, WIDE)[:, :COLS].astype(F32)
-    for j in (1, 3, 2):
-        c_copy(j).wait_recv()
-        mid = mid + part_in[j][:, :COLS].astype(F32)
-    mid_s[...] = mid
-    square = jnp.sum(mid * mid, axis=1, keepdims=True)
-    square_hi = square.astype(BF16).astype(F32)
-    square_lo = square - square_hi
-    lane = lax.broadcasted_iota(jnp.int32, (TOKENS, WIDE - COLS), 1)
-    spare = jnp.where(lane == 0, square_hi, jnp.where(lane == 1, square_lo, 0.0))
-    all_rows = jnp.concatenate([(mid * gain[...]), spare], axis=1).astype(BF16)
+    lane = lax.broadcasted_iota(jnp.int32, (2 * QTOK, WIDE - COLS), 1)
+
+    def rows_of(h):
+        blocks = [(z + 1 + 2 * h) % 4, (z + 2 + 2 * h) % 4]
+        mid = jnp.concatenate([proj[q] + hidden[q][:, :COLS].astype(F32) for q in blocks], axis=0)
+        for j in (1, 3, 2):
+            c_copy(h, j).wait_recv()
+            mid = mid + part_in[h, j].reshape(2 * QTOK, WIDE)[:, :COLS].astype(F32)
+        if h == 1:
+            mid_s[...] = mid[QTOK:]
+        square = jnp.sum(mid * mid, axis=1, keepdims=True)
+        square_hi = square.astype(BF16).astype(F32)
+        square_lo = square - square_hi
+        spare = jnp.where(lane == 0, square_hi, jnp.where(lane == 1, square_lo, 0.0))
+        return jnp.concatenate([(mid * gain[...]), spare], axis=1).astype(BF16)
+
     def e_copy(h, k):
         return remote(
             x_out.at[h, k], x_a.at[h, k], e_s, e_r.at[h * 3 + (k - 1) // 5], peer(k) * 2 + core, z
@@ -239,8 +276,9 @@
         return remote(x_a.at[h, ks], x_b.at[h, ks], e2_s, e2_r.at[h * 4 + n], sib, z)
 
     for h in range(2):
+        all_rows = rows_of(h)
         for first in range(1, XY, 5):
-            rows = mm(pick[h, first : first + 5].reshape(5 * PART, TOKENS), all_rows).astype(BF16)
+            rows = mm(pick[h, first : first + 5].reshape(5 * PART, 2 * QTOK), all_rows).astype(BF16)
             for k in range(first, first + 5):
                 x_out[h, k] = rows[PART * (k - first) : PART * (k - first + 1)]
                 e_copy(h, k).start()
@@ -288,31 +326,27 @@
         f_copy(h).start()
 
     def g_copy(m, q):
-        return remote(y_out.at[m, q], y_in.at[z * XY + xy], g_s, g_r, core * 16 + m, q)
+        return remote(y_out.at[m, q], y_in.at[z * XY + xy], g_s, g_r, core * 16 + m, (z + 1 + q) % 4)
 
     def g_self(m, q):
         return pltpu.make_async_copy(y_out.at[m, q], y_in.at[z * XY + xy], g_own)
 
     def results(h, n):
         group = (dp // 4 % 4 + n) % 4
-        at = pl.ds(pl.multiple_of(group * 4 * COLS, 128), 4 * COLS)
-        y = mm(act_s[0, h], down_v[0, :, at]) + mm(act_s[1, h], down_v[1, :, at])
-        y = y * wcol[PART * h : PART * (h + 1), :1]
+        weight = wcol[PART * h : PART * (h + 1), :1]
         for k in range(4):
-            low = y[:, COLS * k : COLS * k + 128]
-            high = jnp.concatenate(
-                [y[:, COLS * k + 128 : COLS * (k + 1)], jnp.zeros((PART, WIDE - COLS), F32)], axis=1
-            )
+            m = group * 4 + k
+            y = (mm(act_s[0, h], down_p[0, m]) + mm(act_s[1, h], down_p[1, m])) * weight
+            low, high = y[:, :128], y[:, 128:]
             for q in range(2):
                 at_q = slice(CAP * q, CAP * (q + 1))
                 slab = jnp.concatenate([low[at_q], high[at_q]], axis=0)
-                y_out[group * 4 + k, 2 * h + q] = slab.astype(BF16)
-        for i in range(4):
-            for j in range(2):
+                y_out[m, 2 * h + q] = slab.astype(BF16)
+        for q in ((1, 0) if h == 0 else (2, 3)):
+            for i in range(4):
                 m = group * 4 + (dp + i) % 4
-                q = 2 * h + (z + j) % 2
-                if n == 0 and i == 0 and j == 0:
-                    to_self = (core * 16 + m == dp) & (z == q)
+                if n == 0 and i == 0 and q == 3:
+                    to_self = core * 16 + m == dp
 
                     @pl.when(to_self)
                     def _():
@@ -333,25 +367,23 @@
         sums = take_b(sums, 0, g)
     activate(sums, 0)
     sums = take_own(1)
+    f_copy(0).wait_recv()
+    results(0, 3)
     arrive(1, 0)
+    results(0, 2)
+    arrive(1, 1)
+    results(0, 1)
+    arrive(1, 2)
+    results(0, 0)
     sums = take_a(sums, 1, 0)
     sums = take_b(sums, 1, 0)
-    loads[5].wait()
-    w_copy.wait_recv()
-    f_copy(0).wait_recv()
-    results(0, 0)
-    arrive(1, 1)
-    results(0, 1)
-    results(0, 2)
-    arrive(1, 2)
-    results(0, 3)
     sums = take_a(sums, 1, 1)
     sums = take_b(sums, 1, 1)
     sums = take_a(sums, 1, 2)
     sums = take_b(sums, 1, 2)
     activate(sums, 1)
     f_copy(1).wait_recv()
-    for n in range(4):
+    for n in (3, 2, 1, 0):
         results(1, n)
     mine = side == core
 
@@ -371,7 +403,7 @@
     for j in range(4):
         total = total + mm(merge[...], y_in[XY * j : XY * (j + 1)].reshape(XY * 2 * CAP, 128))
     total = jnp.concatenate([total[:QTOK], total[QTOK:, : COLS - 128]], axis=1)
-    out[...] = (mid_s[pl.ds(pl.multiple_of(z * QTOK, QTOK), QTOK), :] + total).astype(BF16)
+    out[...] = (mid_s[...] + total).astype(BF16)
 
     def left(ref, sem):
         remote(ref, ref, sem, w_r, sib, z).wait_send()
@@ -380,7 +412,8 @@
     left(heads_a, a2_s)
     left(hidden.at[pl.ds(0, 3)], hid_s)
     w_copy.wait_send()
-    left(part_in.at[pl.ds(0, 3)], c_s)
+    left(part_in.at[0, pl.ds(0, 3)], c_s)
+    left(part_in.at[0, pl.ds(0, 3)], c_s)
     left(x_out.at[0], e_s)
     left(x_out.at[0, pl.ds(0, 14)], e_s)
     left(x_a, e2_s)
@@ -401,30 +434,38 @@
     w_gate_up, w_down,
 ):
     vmem = pl.BlockSpec(memory_space=pltpu.VMEM)
-    smem = pl.BlockSpec(memory_space=pltpu.SMEM)
     hbm = pl.BlockSpec(memory_space=pl.ANY)
     dma = pltpu.SemaphoreType.DMA
     return pl.pallas_call(
         kernel,
         out_shape=jax.ShapeDtypeStruct((QTOK, COLS), BF16),
-        in_specs=[vmem, vmem, hbm, smem, hbm, hbm, vmem, vmem, vmem, vmem, hbm, hbm],
+        in_specs=[hbm] * 12,
         out_specs=vmem,
         scratch_shapes=[
+            pltpu.VMEM((4, 16, LAT), BF16),
+            pltpu.VMEM((4, LAT), BF16),
+            pltpu.SMEM((2,), jnp.int32),
+            pltpu.VMEM((QTOK, COLS), BF16),
+            pltpu.VMEM((1, COLS), F32),
+            pltpu.VMEM((TOP, TOKENS), jnp.int32),
+            pltpu.VMEM((TOP, TOKENS), F32),
             pltpu.VMEM((2, LAT, MAXLEN), BF16),
             pltpu.VMEM((16, KVL, VH), BF16),
             pltpu.VMEM((COLS, 16 * VH), BF16),
             pltpu.VMEM((2, D, UNITS), BF16),
             pltpu.VMEM((2, UNITS, HALF), BF16),
+            pltpu.VMEM((2, XY, UNITS, WIDE), BF16),
             pltpu.VMEM((XY, 64, VH), BF16),
             pltpu.VMEM((XY, 64, VH), BF16),
             pltpu.VMEM((32 * 64, VH), F32),
-            pltpu.VMEM((TOKENS, WIDE), BF16),
-            pltpu.VMEM((4, TOKENS, WIDE), BF16),
+            pltpu.VMEM((4, QTOK, COLS), F32),
+            pltpu.VMEM((5, QTOK, WIDE), BF16),
+            pltpu.VMEM((2, 4, 2, QTOK, WIDE), BF16),
             pltpu.VMEM((4, QTOK, WIDE), BF16),
-            pltpu.VMEM((2, XY, PART, TOKENS), BF16),
+            pltpu.VMEM((2, XY, PART, 2 * QTOK), BF16),
             pltpu.VMEM((EXPERTS, TOKENS), F32),
             pltpu.VMEM((EXPERTS, TOKENS), F32),
-            pltpu.VMEM((TOKENS, COLS), F32),
+            pltpu.VMEM((QTOK, COLS), F32),
             pltpu.VMEM((ROWS, 128), F32),
             pltpu.VMEM((2 * QTOK, XY * 2 * CAP), BF16),
             pltpu.VMEM((2, XY, PART, WIDE), BF16),
@@ -433,10 +474,10 @@
             pltpu.VMEM((2, 2, PART, UNITS), BF16),
             pltpu.VMEM((XY, 4, 2 * CAP, 128), BF16),
             pltpu.VMEM((4 * XY, 2 * CAP, 128), BF16),
-            dma((6,)),
+            dma((13,)),
             dma, dma, dma, dma,
             dma, dma((3,)), dma, dma((4,)),
-            dma, dma((4,)),
+            dma, dma((8,)),
             dma, dma((6,)), dma, dma((8,)),
             dma((2,)), dma((2,)), dma, dma, dma,
         ],

time: 51.6 us -> 48.4 us (0.938); the launches traced: 50.7 us -> 48.2 us
  Pallas kernels: 49.3 us -> 46.9 us
    pallas_call x1, Pallas kernels: 49.3 us -> 46.9 us  [on_device(): pl.pallas_call(kernel, out_shape=jax.ShapeDtypeStruct((QTOK, COLS), BF16)...]
where the time goes in v4:
time: 48.4 us; the launch traced here: 48.2 us
  Pallas kernels  46.9 us (97%)
  local copies, waits for them, and re-layouts  1.32 us (3%)
    pallas_call x1, Pallas kernels, on_device(): pl.pallas_call(kernel, out_shape=jax.ShapeDtypeStruct((QTOK, COLS), BF16)...  46.9 us
    unnamed x1, local copies, waits for them, and re-layouts  1.32 us

profile of v4, /device:TPU:1, one launch (start us, length us, event | category | flops | bytes accessed | tf_op | source)
XLA Modules:
  0.0 48.2 jit_solution(4466766672157993088)
XLA Ops:
  0.0 46.9 %shard_map.118 = bf16[32,224]{1,0:T(8,128)(2,1)} custom-call(bf16[4,16,576]{2,1,0:T(8,128)(2,1)} %query_h.1, bf16[4,576]{1,0:T(4,128)(2,1)} %new_latent_h.1, bf16[2,576,1024]{2,1,0:T(8,128)(2,1)} %bitcast.5, s32[2]{0:T(128)} %cache_len_h.1, bf16[16,512,128]{2,1,0:T(8,128)(2,1)} %w_uv.1, bf16[224,2048]{1,0:T(8,128)(2,1)} %bitcast.6, ...), custom_call_target="tpu_custom_call" | custom-call | tf_op jit(solution)/shard_map/pallas_call | solution.py:439
  46.9 1.3 %copy.14 = bf16[32,224]{1,0:T(8,128)(2,1)} copy(bf16[32,224]{1,0:T(8,128)(2,1)} %shard_map.118) | data formatting | bytes 28672

commit v5 on v4

--- a/solution.py
+++ b/solution.py
@@ -69,6 +69,9 @@
             src_ref=src, dst_ref=dst, send_sem=send, recv_sem=recv,
             device_id=(to_dp, to_z), device_id_type=MESH,
         )
+
+    def left(ref, sem):
+        remote(ref, ref, sem, w_r, sib, z).wait_send()
 
     barrier = pltpu.get_barrier_semaphore()
     for k in range(1, XY):
@@ -198,12 +201,13 @@
     merge[QTOK:, :] = jnp.where(found & (place % (2 * CAP) >= CAP), 1.0, 0.0).astype(BF16)
 
     def spread_down(which):
+        units = pl.ds(pl.multiple_of(which * UNITS, UNITS), UNITS)
         for m in range(16):
             first, last = COLS * m // 128, (COLS * (m + 1) + 127) // 128
             at = COLS * m - 128 * first
             piece = down_v[which, :, 128 * first : 128 * last][:, at : at + COLS]
-            down_p[which, m, :, :COLS] = piece
-            down_p[which, m, :, COLS:] = jnp.zeros((UNITS, WIDE - COLS), BF16)
+            down_p[m, units, :COLS] = piece
+            down_p[m, units, COLS:] = jnp.zeros((UNITS, WIDE - COLS), BF16)
 
     loads[5].wait()
     spread_down(core)
@@ -243,11 +247,13 @@
 
     def c_copy(h, j):
         blocks = part.at[pl.ds((z + j + 1 + 2 * h) % 4, 2)]
-        return remote(blocks, part_in.at[h, j], c_s, c_r.at[h * 4 + j], dp, zpeer(j))
+        return remote(blocks, part_in.at[h, j], c_s.at[h], c_r.at[h * 4 + j], dp, zpeer(j))
 
     for h in range(2):
         for j in (2, 1, 3):
             c_copy(h, j).start()
+        if h == 0:
+            left(part_in.at[0, pl.ds(0, 3)], c_s.at[0])
     w_copy.wait_recv()
     spread_down(1 - core)
     remote(hidden.at[pl.ds(0, 3)], hidden.at[pl.ds(0, 3)], hid_s, hid_r, dp, zpeer(1)).wait_recv()
@@ -269,7 +275,7 @@
 
     def e_copy(h, k):
         return remote(
-            x_out.at[h, k], x_a.at[h, k], e_s, e_r.at[h * 3 + (k - 1) // 5], peer(k) * 2 + core, z
+            x_out.at[h, k], x_a.at[h, k], e_s.at[h], e_r.at[h * 3 + (k - 1) // 5], peer(k) * 2 + core, z
         )
 
     def e2_copy(h, ks, n):
@@ -277,6 +283,8 @@
 
     for h in range(2):
         all_rows = rows_of(h)
+        if h == 1:
+            left(x_out.at[0, pl.ds(0, 15)], e_s.at[0])
         for first in range(1, XY, 5):
             rows = mm(pick[h, first : first + 5].reshape(5 * PART, 2 * QTOK), all_rows).astype(BF16)
             for k in range(first, first + 5):
@@ -334,9 +342,10 @@
     def results(h, n):
         group = (dp // 4 % 4 + n) % 4
         weight = wcol[PART * h : PART * (h + 1), :1]
+        act = jnp.concatenate([act_s[0, h], act_s[1, h]], axis=1)
         for k in range(4):
             m = group * 4 + k
-            y = (mm(act_s[0, h], down_p[0, m]) + mm(act_s[1, h], down_p[1, m])) * weight
+            y = mm(act, down_p[m]) * weight
             low, high = y[:, :128], y[:, 128:]
             for q in range(2):
                 at_q = slice(CAP * q, CAP * (q + 1))
@@ -390,6 +399,17 @@
     def slabs(count):
         return remote(y_in.at[pl.ds(0, count)], y_in.at[pl.ds(0, count)], g_s, g_r, sib, z)
 
+
+    left(heads_a.at[pl.ds(0, 15)], a_s)
+    left(heads_a, a2_s)
+    left(hidden.at[pl.ds(0, 3)], hid_s)
+    w_copy.wait_send()
+    left(part_in.at[1, pl.ds(0, 3)], c_s.at[1])
+    left(x_out.at[1, pl.ds(0, 15)], e_s.at[1])
+    left(x_a, e2_s)
+    for h in range(2):
+        f_copy(h).wait_send()
+
     @pl.when(mine)
     def _():
         slabs(63).wait_recv()
@@ -404,21 +424,6 @@
         total = total + mm(merge[...], y_in[XY * j : XY * (j + 1)].reshape(XY * 2 * CAP, 128))
     total = jnp.concatenate([total[:QTOK], total[QTOK:, : COLS - 128]], axis=1)
     out[...] = (mid_s[...] + total).astype(BF16)
-
-    def left(ref, sem):
-        remote(ref, ref, sem, w_r, sib, z).wait_send()
-
-    left(heads_a.at[pl.ds(0, 15)], a_s)
-    left(heads_a, a2_s)
-    left(hidden.at[pl.ds(0, 3)], hid_s)
-    w_copy.wait_send()
-    left(part_in.at[0, pl.ds(0, 3)], c_s)
-    left(part_in.at[0, pl.ds(0, 3)], c_s)
-    left(x_out.at[0], e_s)
-    left(x_out.at[0, pl.ds(0, 14)], e_s)
-    left(x_a, e2_s)
-    for h in range(2):
-        f_copy(h).wait_send()
 
     @pl.when(mine)
     def _():
@@ -454,7 +459,7 @@
             pltpu.VMEM((COLS, 16 * VH), BF16),
             pltpu.VMEM((2, D, UNITS), BF16),
             pltpu.VMEM((2, UNITS, HALF), BF16),
-            pltpu.VMEM((2, XY, UNITS, WIDE), BF16),
+            pltpu.VMEM((XY, 2 * UNITS, WIDE), BF16),
             pltpu.VMEM((XY, 64, VH), BF16),
             pltpu.VMEM((XY, 64, VH), BF16),
             pltpu.VMEM((32 * 64, VH), F32),
@@ -477,8 +482,8 @@
             dma((13,)),
             dma, dma, dma, dma,
             dma, dma((3,)), dma, dma((4,)),
-            dma, dma((8,)),
-            dma, dma((6,)), dma, dma((8,)),
+            dma((2,)), dma((8,)),
+            dma((2,)), dma((6,)), dma, dma((8,)),
             dma((2,)), dma((2,)), dma, dma, dma,
         ],
         compiler_params=pltpu.CompilerParams(

time: 48.4 us -> 48.1 us (level)
  no operation moved by 1% of the time
where the time goes in v5:
time: 48.1 us; the launch traced here: 47.9 us
  Pallas kernels  46.6 us (97%)
  local copies, waits for them, and re-layouts  1.32 us (3%)
    pallas_call x1, Pallas kernels, on_device(): pl.pallas_call(kernel, out_shape=jax.ShapeDtypeStruct((QTOK, COLS), BF16)...  46.6 us
    unnamed x1, local copies, waits for them, and re-layouts  1.32 us

profile of v5, /device:TPU:1, one launch (start us, length us, event | category | flops | bytes accessed | tf_op | source)
XLA Modules:
  0.0 47.9 jit_solution(4215804243116778717)
XLA Ops:
  0.0 46.6 %shard_map.118 = bf16[32,224]{1,0:T(8,128)(2,1)} custom-call(bf16[4,16,576]{2,1,0:T(8,128)(2,1)} %query_h.1, bf16[4,576]{1,0:T(4,128)(2,1)} %new_latent_h.1, bf16[2,576,1024]{2,1,0:T(8,128)(2,1)} %bitcast.5, s32[2]{0:T(128)} %cache_len_h.1, bf16[16,512,128]{2,1,0:T(8,128)(2,1)} %w_uv.1, bf16[224,2048]{1,0:T(8,128)(2,1)} %bitcast.6, ...), custom_call_target="tpu_custom_call" | custom-call | tf_op jit(solution)/shard_map/pallas_call | solution.py:444
  46.6 1.3 %copy.14 = bf16[32,224]{1,0:T(8,128)(2,1)} copy(bf16[32,224]{1,0:T(8,128)(2,1)} %shard_map.118) | data formatting | bytes 28672

commit v6 on v5

--- a/solution.py
+++ b/solution.py
@@ -275,7 +275,7 @@
 
     def e_copy(h, k):
         return remote(
-            x_out.at[h, k], x_a.at[h, k], e_s.at[h], e_r.at[h * 3 + (k - 1) // 5], peer(k) * 2 + core, z
+            x_out.at[h, k], x_a.at[h, k], e_s.at[h * 3 + (k - 1) // 5], e_r.at[h * 3 + (k - 1) // 5], peer(k) * 2 + core, z
         )
 
     def e2_copy(h, ks, n):
@@ -284,7 +284,8 @@
     for h in range(2):
         all_rows = rows_of(h)
         if h == 1:
-            left(x_out.at[0, pl.ds(0, 15)], e_s.at[0])
+            for n in range(2):
+                left(x_out.at[0, pl.ds(0, 5)], e_s.at[n])
         for first in range(1, XY, 5):
             rows = mm(pick[h, first : first + 5].reshape(5 * PART, 2 * QTOK), all_rows).astype(BF16)
             for k in range(first, first + 5):
@@ -405,7 +406,8 @@
     left(hidden.at[pl.ds(0, 3)], hid_s)
     w_copy.wait_send()
     left(part_in.at[1, pl.ds(0, 3)], c_s.at[1])
-    left(x_out.at[1, pl.ds(0, 15)], e_s.at[1])
+    for n in range(2, 6):
+        left(x_out.at[1, pl.ds(0, 5)], e_s.at[n])
     left(x_a, e2_s)
     for h in range(2):
         f_copy(h).wait_send()
@@ -483,7 +485,7 @@
             dma, dma, dma, dma,
             dma, dma((3,)), dma, dma((4,)),
             dma((2,)), dma((8,)),
-            dma((2,)), dma((6,)), dma, dma((8,)),
+            dma((6,)), dma((6,)), dma, dma((8,)),
             dma((2,)), dma((2,)), dma, dma, dma,
         ],
         compiler_params=pltpu.CompilerParams(

time: 48.1 us -> 47.9 us (level)
  no operation moved by 1% of the time
where the time goes in v6:
time: 47.9 us; the launch traced here: 47.8 us
  Pallas kernels  46.4 us (97%)
  local copies, waits for them, and re-layouts  1.32 us (3%)
    pallas_call x1, Pallas kernels, on_device(): pl.pallas_call(kernel, out_shape=jax.ShapeDtypeStruct((QTOK, COLS), BF16)...  46.4 us
    unnamed x1, local copies, waits for them, and re-layouts  1.32 us

profile of v6, /device:TPU:1, one launch (start us, length us, event | category | flops | bytes accessed | tf_op | source)
XLA Modules:
  0.0 47.8 jit_solution(8480788677607067105)
XLA Ops:
  0.0 46.4 %shard_map.118 = bf16[32,224]{1,0:T(8,128)(2,1)} custom-call(bf16[4,16,576]{2,1,0:T(8,128)(2,1)} %query_h.1, bf16[4,576]{1,0:T(4,128)(2,1)} %new_latent_h.1, bf16[2,576,1024]{2,1,0:T(8,128)(2,1)} %bitcast.5, s32[2]{0:T(128)} %cache_len_h.1, bf16[16,512,128]{2,1,0:T(8,128)(2,1)} %w_uv.1, bf16[224,2048]{1,0:T(8,128)(2,1)} %bitcast.6, ...), custom_call_target="tpu_custom_call" | custom-call | tf_op jit(solution)/shard_map/pallas_call | solution.py:446
  46.4 1.3 %copy.14 = bf16[32,224]{1,0:T(8,128)(2,1)} copy(bf16[32,224]{1,0:T(8,128)(2,1)} %shard_map.118) | data formatting | bytes 28672
